TPU v7x, 512 devices: a whole 4x8x8 slice. The times are simulated.
512 devices in a mesh: shot: 32 (over y, x), tm: 16 (over z, core).
Axes of the slice: x: 4, y: 8, z: 8, core: 2. Of those that a mesh axis runs over, the one named last changes fastest.
Arguments:
- records: bfloat16 [32, 64, 2048], P('shot', None, 'tm'), may hold values from -6 to 6
- live: int32 [32, 64], P('shot'), may hold values 0 or 1
- dither: int32 [32], replicated, may hold values from 0 to 32, as said below
- designature: bfloat16 [9, 33], replicated, may hold values from -0.375 to 0.375
- first_weights: bfloat16 [64, 30], replicated, may hold values from -1.5 to 1.5
- first_bias: float32 [64], replicated, may hold values from -2.5 to 2.5
- hidden_weights: bfloat16 [3, 64, 192], replicated, may hold values from -0.625 to 0.625
- hidden_bias: float32 [3, 64], replicated, may hold values from -2.5 to 2.5
- out_weights: bfloat16 [64], replicated, may hold values from -0.75 to 0.75
- out_bias: float32 [1], replicated, may hold values from -2.5 to 2.5
- shaping: bfloat16 [9, 33], replicated, may hold values from -0.375 to 0.375
Outputs:
- interference: bfloat16 [32, 64, 2048], P('shot', None, 'tm')
- cleaned: bfloat16 [32, 64, 2048], P('shot', None, 'tm')
Inputs may be any that keep to these rules, and one draw needn't show every extreme that they name: One shot's dither is exactly 32 and one shot's is 0.
All inputs are finite; a program needn't handle non-finite values. No bound on the sum of `live` on one device may be relied on, other than what follows from the above.
Results may differ from a plain program's by a relative error of at most 0.012.
The roundings to bfloat16 on the way count: a program that leaves them out, or rounds other values in their place, can miss the bound.
Values may be sent and summed in bfloat16 or wider, within the bound.
A program may use at most 64 MiB of HBM per device.

v0:
```python
import jax
import jax.numpy as jnp
from jax import lax
from jax.sharding import PartitionSpec as P

HID = 3
FN = 9
FT = 33
SHOT_TAPS = 5
DMAX = 32


def extended_2(array, sides, width):
    for axis, dim in sides:
        devices, length = (lax.axis_size(axis), array.shape[dim])
        up = [(i, (i + 1) % devices) for i in range(devices - 1)]
        down = [(j, i) for i, j in up]
        last = lax.slice_in_dim(array, length - width, length, axis=dim)
        leading = lax.slice_in_dim(array, 0, width, axis=dim)
        before = lax.ppermute(last, axis, up)
        after = lax.ppermute(leading, axis, down)
        array = jnp.concatenate([before, array, after], axis=dim)
    return array


def from_behind(value, axis, steps):
    count = lax.axis_size(axis)
    leading, last = (max(0, -steps), min(count, count - steps))
    return lax.ppermute(value, axis, [(source, source + steps) for source in range(leading, last)])


def apply_taps(rimmed, taps):
    shots_here, nodes, length = rimmed.shape
    samples = length - (FT - 1)
    node_pad = jnp.pad(rimmed, ((0, 0), (FN // 2, FN // 2), (0, 0)))
    shifted = jnp.stack([node_pad[:, offset : offset + nodes, :] for offset in range(FN)], axis=2)
    partial_rows = jnp.einsum("snal,ab->snbl", shifted, taps, preferred_element_type=jnp.float32)
    total_sum = partial_rows[:, :, 0, 0:samples]
    for shift in range(1, FT):
        total_sum = total_sum + partial_rows[:, :, shift, shift : shift + samples]
    return total_sum


def valid_mask(width, samples, first_sample, total):
    margin = (width - samples) // 2
    positions = first_sample + jnp.arange(width, dtype=jnp.int32) - margin
    return (positions >= 0) & (positions < total)


def predict(
    gather_rows,
    dither_rows,
    first_weights,
    first_bias,
    hidden_weights,
    hidden_bias,
    out_weights,
    out_bias,
    samples,
    first_sample,
    total,
):
    rows_in = gather_rows.shape[1]
    rows_out = rows_in - 2 * (SHOT_TAPS // 2)
    reach_full = 2 ** (HID + 1) - 1
    extended = extended_2(gather_rows, (("tm", 2),), DMAX + reach_full)
    span = samples + 2 * reach_full
    direct = extended[:, :, DMAX : DMAX + span]
    shift_rows = jax.vmap(lambda row, delay: lax.dynamic_slice_in_dim(row, DMAX + delay, span))
    retimed = jax.vmap(shift_rows, in_axes=(0, None))(extended, dither_rows)
    inputs = jnp.stack([direct, retimed])
    inputs = jnp.where(
        valid_mask(span, samples, first_sample, total)[None, None, None, :],
        inputs,
        jnp.zeros_like(inputs),
    )
    width = span - 2
    columns = jnp.stack(
        [
            inputs[channel, :, offset : offset + rows_out, shift : shift + width]
            for channel in range(2)
            for offset in range(SHOT_TAPS)
            for shift in range(3)
        ]
    )
    summed = jnp.einsum("of,fgst->ogst", first_weights, columns, preferred_element_type=jnp.float32)
    summed = summed + first_bias[:, None, None, None]
    keep_time = valid_mask(width, samples, first_sample, total)[None, None, None, :]
    active = jnp.where(keep_time, jax.nn.relu(summed), 0.0).astype(jnp.bfloat16)
    for layer in range(HID):
        dilation = 2 ** (layer + 1)
        width = active.shape[3] - 2 * dilation
        stacked = jnp.concatenate(
            [active[:, :, :, shift * dilation : shift * dilation + width] for shift in range(3)],
            axis=0,
        )
        summed = jnp.einsum(
            "of,fgst->ogst", hidden_weights[layer], stacked, preferred_element_type=jnp.float32
        )
        summed = summed + hidden_bias[layer][:, None, None, None]
        keep_time = valid_mask(width, samples, first_sample, total)[None, None, None, :]
        active = jnp.where(keep_time, jax.nn.relu(summed), 0.0).astype(jnp.bfloat16)
    result = (
        jnp.einsum("c,cgst->gst", out_weights, active, preferred_element_type=jnp.float32)
        + out_bias[0]
    )
    return result.astype(jnp.bfloat16)


def local(
    records,
    live,
    dither,
    designature,
    first_weights,
    first_bias,
    hidden_weights,
    hidden_bias,
    out_weights,
    out_bias,
    shaping,
):
    samples = records.shape[2]
    shots_here = records.shape[0]
    total = samples * lax.axis_size("tm")
    first_sample = lax.axis_index("tm") * samples
    margin_rows = SHOT_TAPS // 2
    keep = live[:, :, None] > 0
    masked = jnp.where(keep, records, jnp.zeros_like(records))
    rimmed = extended_2(masked, (("tm", 2),), FT // 2)
    filtered = jnp.where(keep, apply_taps(rimmed, designature), 0.0).astype(jnp.bfloat16)
    padded_dither = jnp.pad(dither, ((margin_rows, margin_rows),))
    weights = (first_weights, first_bias, hidden_weights, hidden_bias, out_weights, out_bias)
    reach_devs = (margin_rows + shots_here - 1) // shots_here
    offsets = list(range(reach_devs, 0, -1)) + list(range(-1, -reach_devs - 1, -1))
    moved = {}
    for offset in offsets:
        moved[offset] = from_behind(filtered, "shot", offset)
    before = [moved[offset] for offset in range(reach_devs, 0, -1)]
    after = [moved[offset] for offset in range(-1, -reach_devs - 1, -1)]
    joined = jnp.concatenate(before + [filtered] + after, axis=0)
    near_dither = lax.dynamic_slice_in_dim(
        padded_dither, lax.axis_index("shot") * shots_here, shots_here + 2 * margin_rows
    )
    by_node = jnp.transpose(joined, (1, 0, 2))
    predicted = predict(by_node, near_dither, *weights, samples, first_sample, total)
    returned = jnp.transpose(predicted, (1, 0, 2))
    interference = jnp.where(keep, returned, jnp.zeros_like(returned))
    deblended = (filtered.astype(jnp.float32) - interference.astype(jnp.float32)).astype(
        jnp.bfloat16
    )
    rimmed_again = extended_2(deblended, (("tm", 2),), FT // 2)
    cleaned = jnp.where(keep, apply_taps(rimmed_again, shaping), 0.0).astype(jnp.bfloat16)
    return (interference, cleaned)


def solution(mesh):
    in_specs = (P("shot", None, "tm"), P("shot", None), P(), P(), P(), P(), P(), P(), P(), P(), P())
    out_specs = (P("shot", None, "tm"), P("shot", None, "tm"))
    return jax.shard_map(local, mesh=mesh, in_specs=in_specs, out_specs=out_specs, check_vma=False)
```

profile of v0, /device:TPU:225, one launch (start us, length us, event | category | flops | bytes accessed | tf_op | source)
XLA Modules:
  0.0 78.8 jit_solution(12155127694052957441)
XLA Ops:
  2.2 5.8 %collective-permute-start = (bf16[1,64,16]{2,1,0:T(8,128)(2,1)S(1)}, bf16[1,64,16]{2,1,0:T(8,128)(2,1)S(1)}, u32[]{:S(2)}, u32[]{:S(2)}) collective-permute-start(bf16[1,64,16]{2,1,0:T(8,128)(2,1)S(1)} %get-tuple-element.58), channel_id=1, source_target_pairs={{0,1},{1,2},{2,3},{3,4},{4,5},{5,6},{6,7},{7,8},{8,9},{9,10},{10,1... | collective-permute-start | bytes 6152 | tf_op jit(solution)/shard_map/ppermute | solution.py:20
  8.0 1.9 %collective-permute-start.1 = (bf16[1,64,16]{2,1,0:T(8,128)(2,1)S(1)}, bf16[1,64,16]{2,1,0:T(8,128)(2,1)S(1)}, u32[]{:S(2)}, u32[]{:S(2)}) collective-permute-start(bf16[1,64,16]{2,1,0:T(8,128)(2,1)S(1)} %get-tuple-element.59), channel_id=1, source_target_pairs={{1,0},{2,1},{3,2},{4,3},{5,4},{6,5},{7,6},{8,7},{9,8},{10,9},{11,1... | collective-permute-start | bytes 6152 | tf_op jit(solution)/shard_map/ppermute | solution.py:21
  9.9 1.3 %slice_bitcast_fusion.25 = (f32[64]{0:T(128)}, f32[64]{0:T(128)S(1)}, f32[64]{0:T(128)S(1)}) fusion(f32[3,64]{1,0:T(4,128)} %param.18), kind=kLoop, calls=%fused_computation.207 | loop fusion | bytes 1536 | tf_op jit(solution)/shard_map/add | solution.py:100
  11.3 3.0 %collective-permute-done.1 = bf16[1,64,16]{2,1,0:T(8,128)(2,1)S(1)} collective-permute-done((bf16[1,64,16]{2,1,0:T(8,128)(2,1)S(1)}, bf16[1,64,16]{2,1,0:T(8,128)(2,1)S(1)}, u32[]{:S(2)}, u32[]{:S(2)}) %collective-permute-start.1) | collective-permute-done | bytes 2080 | tf_op jit(solution)/shard_map/ppermute | solution.py:21
  16.0 1.2 %convolution_bitcast_fusion = f32[1,64,33,160]{3,2,1,0:T(8,128)S(1)} fusion(bf16[1,64,9,160]{3,2,1,0:T(8,128)(2,1)S(1)} %stack.81, bf16[9,33]{1,0:T(8,128)(2,1)} %param.14), kind=kOutput, calls=%fused_computation.26 | convolution fusion | flops 6082560 | bytes 1536594 | tf_op jit(solution)/shard_map/snal,ab->snbl/dot_general | solution.py:37
  17.2 1.4 %fusion.102 = (f32[1,64,1,128]{3,2,1,0:T(1,128)S(1)}, f32[1,64,1,128]{3,2,1,0:T(1,128)S(1)}, f32[1,64,1,128]{3,2,1,0:T(1,128)S(1)}, f32[1,64,1,128]{3,2,1,0:T(1,...) fusion(f32[1,64,33,160]{3,2,1,0:T(8,128)S(1)} %convolution_bitc, ...), kind=kLoop, calls=%fused_computation.215 | loop fusion | bytes 1245184 | tf_op jit(solution)/shard_map/slice | solution.py:40
  20.3 4.6 %collective-permute-start.2 = (bf16[1,64,128]{2,1,0:T(8,128)(2,1)S(1)}, bf16[1,64,128]{2,1,0:T(8,128)(2,1)S(1)}, u32[]{:S(2)}, u32[]{:S(2)}) collective-permute-start(bf16[1,64,128]{2,1,0:T(8,128)(2,1)S(1)} %get-tuple-element.2), channel_id=1, source_target_pairs={{0,32},{16,48},{32,64},{48,80},{64,96},{80,112},{96,128},{112,144}... | collective-permute-start | bytes 49160 | tf_op jit(solution)/shard_map/ppermute | solution.py:29
  25.4 2.2 %collective-permute-start.3 = (bf16[1,64,128]{2,1,0:T(8,128)(2,1)S(1)}, bf16[1,64,128]{2,1,0:T(8,128)(2,1)S(1)}, u32[]{:S(2)}, u32[]{:S(2)}) collective-permute-start(bf16[1,64,128]{2,1,0:T(8,128)(2,1)S(1)} %get-tuple-element.2), channel_id=1, source_target_pairs={{0,16},{16,32},{32,48},{48,64},{64,80},{80,96},{96,112},{112,128},... | collective-permute-start | bytes 49160 | tf_op jit(solution)/shard_map/ppermute | solution.py:29
  27.7 6.4 %collective-permute-start.4 = (bf16[1,64,128]{2,1,0:T(8,128)(2,1)S(1)}, bf16[1,64,128]{2,1,0:T(8,128)(2,1)S(1)}, u32[]{:S(2)}, u32[]{:S(2)}) collective-permute-start(bf16[1,64,128]{2,1,0:T(8,128)(2,1)S(1)} %get-tuple-element.2), channel_id=1, source_target_pairs={{16,0},{32,16},{48,32},{64,48},{80,64},{96,80},{112,96},{128,112},... | collective-permute-start | bytes 49160 | tf_op jit(solution)/shard_map/ppermute | solution.py:29
  34.1 1.9 %collective-permute-start.5 = (bf16[1,64,128]{2,1,0:T(8,128)(2,1)S(1)}, bf16[1,64,128]{2,1,0:T(8,128)(2,1)S(1)}, u32[]{:S(2)}, u32[]{:S(2)}) collective-permute-start(bf16[1,64,128]{2,1,0:T(8,128)(2,1)S(1)} %get-tuple-element.2), channel_id=1, source_target_pairs={{32,0},{48,16},{64,32},{80,48},{96,64},{112,80},{128,96},{144,112}... | collective-permute-start | bytes 49160 | tf_op jit(solution)/shard_map/ppermute | solution.py:29
  36.1 4.0 %collective-permute-done.5 = bf16[1,64,128]{2,1,0:T(8,128)(2,1)S(1)} collective-permute-done((bf16[1,64,128]{2,1,0:T(8,128)(2,1)S(1)}, bf16[1,64,128]{2,1,0:T(8,128)(2,1)S(1)}, u32[]{:S(2)}, u32[]{:S(2)}) %collective-permute-start.5) | collective-permute-done | bytes 16416 | tf_op jit(solution)/shard_map/ppermute | solution.py:29
  40.1 3.9 %collective-permute-start.6 = (bf16[64,5,47]{2,0,1:T(8,128)(2,1)S(1)}, bf16[64,5,47]{2,0,1:T(8,128)(2,1)S(1)}, u32[]{:S(2)}, u32[]{:S(2)}) collective-permute-start(bf16[64,5,47]{2,0,1:T(8,128)(2,1)S(1)} %get-tuple-element.46), channel_id=1, source_target_pairs={{0,1},{1,2},{2,3},{3,4},{4,5},{5,6},{6,7},{7,8},{8,9},{9,10},{10,1... | collective-permute-start | bytes 90248 | tf_op jit(solution)/shard_map/ppermute | solution.py:20
  44.1 2.1 %collective-permute-start.7 = (bf16[64,5,47]{2,0,1:T(8,128)(2,1)S(1)}, bf16[64,5,47]{2,0,1:T(8,128)(2,1)S(1)}, u32[]{:S(2)}, u32[]{:S(2)}) collective-permute-start(bf16[64,5,47]{2,0,1:T(8,128)(2,1)S(1)} %get-tuple-element.47), channel_id=1, source_target_pairs={{1,0},{2,1},{3,2},{4,3},{5,4},{6,5},{7,6},{8,7},{9,8},{10,9},{11,1... | collective-permute-start | bytes 90248 | tf_op jit(solution)/shard_map/ppermute | solution.py:21
  47.0 4.1 %collective-permute-done.7 = bf16[64,5,47]{2,0,1:T(8,128)(2,1)S(1)} collective-permute-done((bf16[64,5,47]{2,0,1:T(8,128)(2,1)S(1)}, bf16[64,5,47]{2,0,1:T(8,128)(2,1)S(1)}, u32[]{:S(2)}, u32[]{:S(2)}) %collective-permute-start.7) | collective-permute-done | bytes 30112 | tf_op jit(solution)/shard_map/ppermute | solution.py:21
  51.6 1.5 %gather_fusion = bf16[5,64,158]{1,0,2:T(8,128)(2,1)S(1)} fusion(bf16[64,5,222]{0,1,2:T(8,128)(2,1)S(1)} %copy.198, s32[5]{0:T(128)S(1)} %fusion.95), kind=kCustom, calls=%fused_computation | custom fusion | bytes 202280 | tf_op jit(solution)/shard_map/vmap(vmap())/gather | solution.py:69
  56.4 1.7 %fusion.106 = (bf16[64,64,1,152]{3,0,1,2:T(8,128)(2,1)S(1)}, bf16[64,64,1,152]{3,0,1,2:T(8,128)(2,1)S(1)}, bf16[64,64,1,152]{3,0,1,2:T(8,128)(2,1)S(1)}) fusion(bf16[64,64,1,156]{3,0,1,2:T(8,128)(2,1)S(1)} %fusion.17), kind=kLoop, calls=%fused_computation.219 | loop fusion | bytes 7471104 | tf_op jit(solution)/shard_map/slice | solution.py:94
  58.2 2.0 %fusion.15 = bf16[64,64,1,152]{3,0,1,2:T(8,128)(2,1)S(1)} fusion(f32[64]{0:T(128)S(1)} %get-tuple-element.61, pred[152]{0:T(512)(128)(4,1)S(1)} %compare_and_fusion.2, bf16[64,64,1,152]{3,0,1,2:T(8,128)(2,1)S(1)} %get-tuple-element.44, bf16[64,64,1,152]{3,0,1,2:T(8,128)(2,1)S(1)} %get-tuple-element.45, bf16[64,64,1,152]{3,0,1,2:T(8,128)(2,1)S(1)} %get-tuple-element.43, ...), kind=kOutput, calls=%fused_computation.23 | convolution fusion | flops 252772352 | bytes 7570432 | tf_op jit(solution)/shard_map/of,fgst->ogst/dot_general | solution.py:97
  60.2 1.7 %fusion.105 = (bf16[64,64,1,144]{3,0,1,2:T(8,128)(2,1)S(1)}, bf16[64,64,1,144]{3,0,1,2:T(8,128)(2,1)S(1)}, bf16[64,64,1,144]{3,0,1,2:T(8,128)(2,1)S(1)}) fusion(bf16[64,64,1,152]{3,0,1,2:T(8,128)(2,1)S(1)} %fusion.15), kind=kLoop, calls=%fused_computation.218 | loop fusion | bytes 7077888 | tf_op jit(solution)/shard_map/slice | solution.py:94
  61.9 2.1 %fusion.16 = bf16[64,64,1,144]{3,0,1,2:T(8,128)(2,1)S(1)} fusion(f32[64]{0:T(128)S(1)} %get-tuple-element.62, pred[144]{0:T(512)(128)(4,1)S(1)} %compare_and_fusion.3, bf16[64,64,1,144]{3,0,1,2:T(8,128)(2,1)S(1)} %get-tuple-element.41, bf16[64,64,1,144]{3,0,1,2:T(8,128)(2,1)S(1)} %get-tuple-element.42, bf16[64,64,1,144]{3,0,1,2:T(8,128)(2,1)S(1)} %get-tuple-element.40, ...), kind=kOutput, calls=%fused_computation.24 | convolution fusion | flops 239468544 | bytes 7504896 | tf_op jit(solution)/shard_map/of,fgst->ogst/dot_general | solution.py:97
  64.8 2.2 %fusion.19 = f32[1,64,128]{2,0,1:T(1,128)} fusion(bf16[64,64,1,128]{3,0,1,2:T(8,128)(2,1)S(1)} %get-tuple-element.38, bf16[64,64,1,128]{3,0,1,2:T(8,128)(2,1)S(1)} %get-tuple-element.39, bf16[64,64,1,128]{3,0,1,2:T(8,128)(2,1)S(1)} %get-tuple-element.37, f32[64]{0:T(128)} %get-tuple-element.60, pred[128]{0:T(512)(128)(4,1)} %compare_and_fusion.4, ...), kind=kOutput, calls=%fused_computation.29 | convolution fusion | flops 213909504 | bytes 3212800 | tf_op jit(solution)/shard_map/c,cgst->gst/dot_general | solution.py:104
  68.1 1.9 %collective-permute-start.8 = (bf16[1,64,16]{2,1,0:T(8,128)(2,1)S(1)}, bf16[1,64,16]{2,1,0:T(8,128)(2,1)S(1)}, u32[]{:S(2)}, u32[]{:S(2)}) collective-permute-start(bf16[1,64,16]{2,1,0:T(8,128)(2,1)S(1)} %get-tuple-element.56), channel_id=1, source_target_pairs={{0,1},{1,2},{2,3},{3,4},{4,5},{5,6},{6,7},{7,8},{8,9},{9,10},{10,1... | collective-permute-start | bytes 6152 | tf_op jit(solution)/shard_map/ppermute | solution.py:20
  70.0 2.4 %collective-permute-start.9 = (bf16[1,64,16]{2,1,0:T(8,128)(2,1)S(1)}, bf16[1,64,16]{2,1,0:T(8,128)(2,1)S(1)}, u32[]{:S(2)}, u32[]{:S(2)}) collective-permute-start(bf16[1,64,16]{2,1,0:T(8,128)(2,1)S(1)} %get-tuple-element.57), channel_id=1, source_target_pairs={{1,0},{2,1},{3,2},{4,3},{5,4},{6,5},{7,6},{8,7},{9,8},{10,9},{11,1... | collective-permute-start | bytes 6152 | tf_op jit(solution)/shard_map/ppermute | solution.py:21
  72.4 1.4 %fusion.101 = bf16[1,64,128]{2,1,0:T(8,128)(2,1)} fusion(f32[64,128]{1,0:T(8,128)} %bitcast.468, f32[]{:T(128)} %bitcast.411, pred[64]{0:T(512)(128)(4,1)S(1)} %compare_bitcast_fusion), kind=kLoop, calls=%fused_computation.214 | loop fusion | flops 24576 | bytes 49220 | tf_op jit(solution)/shard_map/jit(_where)/select_n | solution.py:148
  73.9 2.4 %collective-permute-done.9 = bf16[1,64,16]{2,1,0:T(8,128)(2,1)S(1)} collective-permute-done((bf16[1,64,16]{2,1,0:T(8,128)(2,1)S(1)}, bf16[1,64,16]{2,1,0:T(8,128)(2,1)S(1)}, u32[]{:S(2)}, u32[]{:S(2)}) %collective-permute-start.9) | collective-permute-done | bytes 2080 | tf_op jit(solution)/shard_map/ppermute | solution.py:21
  (106 shorter events, 13.5 us)
Async XLA Ops:
  0.6 54.6 %copy-start = (bf16[64,30]{0,1:T(8,128)(2,1)S(1)}, bf16[64,30]{0,1:T(8,128)(2,1)}, u32[]{:S(2)}) copy-start(bf16[64,30]{0,1:T(8,128)(2,1)} %param.15) | copy-start | bytes 11524
  2.2 9.1 %collective-permute-start = (bf16[1,64,16]{2,1,0:T(8,128)(2,1)S(1)}, bf16[1,64,16]{2,1,0:T(8,128)(2,1)S(1)}, u32[]{:S(2)}, u32[]{:S(2)}) collective-permute-start(bf16[1,64,16]{2,1,0:T(8,128)(2,1)S(1)} %get-tuple-element.58), channel_id=1, source_target_pairs={{0,1},{1,2},{2,3},{3,4},{4,5},{5,6},{6,7},{7,8},{8,9},{9,10},{10,1... | collective-permute-start | bytes 6152 | tf_op jit(solution)/shard_map/ppermute | solution.py:20
  8.0 6.3 %collective-permute-start.1 = (bf16[1,64,16]{2,1,0:T(8,128)(2,1)S(1)}, bf16[1,64,16]{2,1,0:T(8,128)(2,1)S(1)}, u32[]{:S(2)}, u32[]{:S(2)}) collective-permute-start(bf16[1,64,16]{2,1,0:T(8,128)(2,1)S(1)} %get-tuple-element.59), channel_id=1, source_target_pairs={{1,0},{2,1},{3,2},{4,3},{5,4},{6,5},{7,6},{8,7},{9,8},{10,9},{11,1... | collective-permute-start | bytes 6152 | tf_op jit(solution)/shard_map/ppermute | solution.py:21
  17.2 29.0 %copy-start.7 = (s32[32]{0:T(128)S(1)}, s32[32]{0:T(128)}, u32[]{:S(2)}) copy-start(s32[32]{0:T(128)} %param.13) | copy-start | bytes 388
  18.6 1.0 %copy-start.1 = (f32[1,64,1,128]{3,2,1,0:T(1,128)}, f32[1,64,1,128]{3,2,1,0:T(1,128)S(1)}, u32[]{:S(2)}) copy-start(f32[1,64,1,128]{3,2,1,0:T(1,128)S(1)} %get-tuple-element.17) | copy-start | bytes 98308
  18.6 1.7 %copy-start.2 = (f32[1,64,1,128]{3,2,1,0:T(1,128)}, f32[1,64,1,128]{3,2,1,0:T(1,128)S(1)}, u32[]{:S(2)}) copy-start(f32[1,64,1,128]{3,2,1,0:T(1,128)S(1)} %get-tuple-element.18) | copy-start | bytes 98308
  19.5 0.7 copy-start.3
  19.5 5.4 %copy-start.4 = (f32[1,64,1,128]{3,2,1,0:T(1,128)}, f32[1,64,1,128]{3,2,1,0:T(1,128)S(1)}, u32[]{:S(2)}) copy-start(f32[1,64,1,128]{3,2,1,0:T(1,128)S(1)} %get-tuple-element.36) | copy-start | bytes 98308
  20.3 15.7 %collective-permute-start.2 = (bf16[1,64,128]{2,1,0:T(8,128)(2,1)S(1)}, bf16[1,64,128]{2,1,0:T(8,128)(2,1)S(1)}, u32[]{:S(2)}, u32[]{:S(2)}) collective-permute-start(bf16[1,64,128]{2,1,0:T(8,128)(2,1)S(1)} %get-tuple-element.2), channel_id=1, source_target_pairs={{0,32},{16,48},{32,64},{48,80},{64,96},{80,112},{96,128},{112,144}... | collective-permute-start | bytes 49160 | tf_op jit(solution)/shard_map/ppermute | solution.py:29
  25.4 10.6 %collective-permute-start.3 = (bf16[1,64,128]{2,1,0:T(8,128)(2,1)S(1)}, bf16[1,64,128]{2,1,0:T(8,128)(2,1)S(1)}, u32[]{:S(2)}, u32[]{:S(2)}) collective-permute-start(bf16[1,64,128]{2,1,0:T(8,128)(2,1)S(1)} %get-tuple-element.2), channel_id=1, source_target_pairs={{0,16},{16,32},{32,48},{48,64},{64,80},{80,96},{96,112},{112,128},... | collective-permute-start | bytes 49160 | tf_op jit(solution)/shard_map/ppermute | solution.py:29
  27.7 8.4 %collective-permute-start.4 = (bf16[1,64,128]{2,1,0:T(8,128)(2,1)S(1)}, bf16[1,64,128]{2,1,0:T(8,128)(2,1)S(1)}, u32[]{:S(2)}, u32[]{:S(2)}) collective-permute-start(bf16[1,64,128]{2,1,0:T(8,128)(2,1)S(1)} %get-tuple-element.2), channel_id=1, source_target_pairs={{16,0},{32,16},{48,32},{64,48},{80,64},{96,80},{112,96},{128,112},... | collective-permute-start | bytes 49160 | tf_op jit(solution)/shard_map/ppermute | solution.py:29
  34.1 6.0 %collective-permute-start.5 = (bf16[1,64,128]{2,1,0:T(8,128)(2,1)S(1)}, bf16[1,64,128]{2,1,0:T(8,128)(2,1)S(1)}, u32[]{:S(2)}, u32[]{:S(2)}) collective-permute-start(bf16[1,64,128]{2,1,0:T(8,128)(2,1)S(1)} %get-tuple-element.2), channel_id=1, source_target_pairs={{32,0},{48,16},{64,32},{80,48},{96,64},{112,80},{128,96},{144,112}... | collective-permute-start | bytes 49160 | tf_op jit(solution)/shard_map/ppermute | solution.py:29
  40.1 6.8 %collective-permute-start.6 = (bf16[64,5,47]{2,0,1:T(8,128)(2,1)S(1)}, bf16[64,5,47]{2,0,1:T(8,128)(2,1)S(1)}, u32[]{:S(2)}, u32[]{:S(2)}) collective-permute-start(bf16[64,5,47]{2,0,1:T(8,128)(2,1)S(1)} %get-tuple-element.46), channel_id=1, source_target_pairs={{0,1},{1,2},{2,3},{3,4},{4,5},{5,6},{6,7},{7,8},{8,9},{9,10},{10,1... | collective-permute-start | bytes 90248 | tf_op jit(solution)/shard_map/ppermute | solution.py:20
  44.1 7.0 %collective-permute-start.7 = (bf16[64,5,47]{2,0,1:T(8,128)(2,1)S(1)}, bf16[64,5,47]{2,0,1:T(8,128)(2,1)S(1)}, u32[]{:S(2)}, u32[]{:S(2)}) collective-permute-start(bf16[64,5,47]{2,0,1:T(8,128)(2,1)S(1)} %get-tuple-element.47), channel_id=1, source_target_pairs={{1,0},{2,1},{3,2},{4,3},{5,4},{6,5},{7,6},{8,7},{9,8},{10,9},{11,1... | collective-permute-start | bytes 90248 | tf_op jit(solution)/shard_map/ppermute | solution.py:21
  51.6 3.6 %copy-start.8 = (f32[64]{0:T(128)S(1)}, f32[64]{0:T(128)}, u32[]{:S(2)}) copy-start(f32[64]{0:T(128)} %param.16) | copy-start | bytes 772
  56.4 1.7 %copy-start.6 = (bf16[3,64,192]{2,1,0:T(8,128)(2,1)S(1)}, bf16[3,64,192]{2,1,0:T(8,128)(2,1)}, u32[]{:S(2)}) copy-start(bf16[3,64,192]{2,1,0:T(8,128)(2,1)} %param.17) | copy-start | bytes 221188
  64.8 11.7 %copy-start.5 = (bf16[9,33]{1,0:T(8,128)(2,1)S(1)}, bf16[9,33]{1,0:T(8,128)(2,1)}, u32[]{:S(2)}) copy-start(bf16[9,33]{1,0:T(8,128)(2,1)} %param.21) | copy-start | bytes 1786
  68.1 5.8 %collective-permute-start.8 = (bf16[1,64,16]{2,1,0:T(8,128)(2,1)S(1)}, bf16[1,64,16]{2,1,0:T(8,128)(2,1)S(1)}, u32[]{:S(2)}, u32[]{:S(2)}) collective-permute-start(bf16[1,64,16]{2,1,0:T(8,128)(2,1)S(1)} %get-tuple-element.56), channel_id=1, source_target_pairs={{0,1},{1,2},{2,3},{3,4},{4,5},{5,6},{6,7},{7,8},{8,9},{9,10},{10,1... | collective-permute-start | bytes 6152 | tf_op jit(solution)/shard_map/ppermute | solution.py:20
  70.0 6.3 %collective-permute-start.9 = (bf16[1,64,16]{2,1,0:T(8,128)(2,1)S(1)}, bf16[1,64,16]{2,1,0:T(8,128)(2,1)S(1)}, u32[]{:S(2)}, u32[]{:S(2)}) collective-permute-start(bf16[1,64,16]{2,1,0:T(8,128)(2,1)S(1)} %get-tuple-element.57), channel_id=1, source_target_pairs={{1,0},{2,1},{3,2},{4,3},{5,4},{6,5},{7,6},{8,7},{9,8},{10,9},{11,1... | collective-permute-start | bytes 6152 | tf_op jit(solution)/shard_map/ppermute | solution.py:21
where the time goes:
time: 79.5 us; the launch traced here: 78.8 us
  starting transfers between devices  33.2 us (42%)
  local copies, waits for them, and re-layouts  14.3 us (18%)
  waiting for transfers between devices  13.5 us (17%)
  matrix products  9.32 us (12%)
  other arithmetic  6.6 us (8%)
  between operations  1.94 us (2%)
    ppermute x4, starting transfers between devices, from_behind(): lax.ppermute(value, axis, [(source, source + steps) for source in range(l...  15.1 us
    ppermute x3, starting transfers between devices, extended_2(): before = lax.ppermute(last, axis, up)  11.6 us
    ppermute x3, waiting for transfers between devices, extended_2(): after = lax.ppermute(leading, axis, down)  9.48 us
    ppermute x3, starting transfers between devices, extended_2(): after = lax.ppermute(leading, axis, down)  6.43 us
    slice x3, local copies, waits for them, and re-layouts, predict(): active[:, :, :, shift * dilation:shift * dilation + width]  4.26 us
    dot_general x2, matrix products, predict(): jnp.einsum('of,fgst->ogst', hidden_weights[layer], stacked, preferred_ele...  4.11 us
    ppermute x4, waiting for transfers between devices, from_behind(): lax.ppermute(value, axis, [(source, source + steps) for source in range(l...  3.98 us
    dot_general x1, matrix products, predict(): jnp.einsum('c,cgst->gst', out_weights, active, preferred_element_type=jnp...  2.24 us
  transfers between devices with their start and end apart: 10, of which 4 were waited for; matrix products, arithmetic and copies ran while one was open for 4% of the time, Pallas kernels for 0%

commit v1 on v0

v1 whole, which is shorter than its diff:
```python
import functools

import jax
import jax.numpy as jnp
from jax import lax
from jax.experimental import pallas as pl
from jax.experimental.pallas import tpu as pltpu
from jax.sharding import PartitionSpec as P

HID = 3
FN = 9
FT = 33
SHOT_TAPS = 5
CH = 64
N = 64
L = 128
GAP = 24
GROUPS = 12
US = 8 * GROUPS
SLOT = {0: 0, -1: 1, 1: 2, -2: 3, 2: 4}
ORDER = (-1, 1, -2, 2)
MESH = pl.DeviceIdType.MESH
BF = jnp.bfloat16
F32 = jnp.float32


def iota(shape, dim):
    return lax.broadcasted_iota(jnp.int32, shape, dim)


def dot_nn(a, b):
    return jnp.dot(a, b, preferred_element_type=F32)


def dot_nt(a, b):
    return lax.dot_general(a, b, (((1,), (1,)), ((), ())), preferred_element_type=F32)


def circulants(taps, store):
    pick = iota((FT, L), 0) == ((FT // 2 - iota((FT, L), 1)) & (L - 1))
    rows = dot_nn(taps, pick.astype(BF))
    near = jnp.abs(iota((L, L), 0) - iota((L, L), 1)) <= L // 2
    for a in range(FN):
        full = jnp.broadcast_to(rows[a : a + 1, :], (L, L))
        full = pltpu.roll(full, 0, 1, stride=1, stride_axis=0)
        store(a, jnp.where(near, full, 0.0).astype(BF), jnp.where(near, 0.0, full).astype(BF))


def kernel(
    shots,
    tms,
    rec,
    live,
    dith,
    des,
    fw,
    fb,
    hw,
    hb,
    ow,
    ob,
    shp,
    inter_out,
    clean_out,
    blk,
    live_in,
    xs,
    c1,
    c2,
    w0,
    wh,
    wo,
    b0s,
    planes,
    gs,
    a0,
    a1,
    a2,
    ds,
    shot_send,
    shot_recv,
    live_send,
    live_recv,
    tm_send,
    tm_recv,
):
    s, z = lax.axis_index("shot"), lax.axis_index("tm")
    z_up, z_down = lax.rem(z + 1, tms), lax.rem(z + tms - 1, tms)

    def shot_at(offset):
        return lax.rem(s + offset + shots, shots)

    barrier = pltpu.get_barrier_semaphore()
    for offset in ORDER:
        pl.semaphore_signal(barrier, inc=1, device_id=(shot_at(offset), z), device_id_type=MESH)
    for other in (z_up, z_down):
        pl.semaphore_signal(barrier, inc=1, device_id=(s, other), device_id_type=MESH)
    pl.semaphore_wait(barrier, 6)

    def send(src, dst, send_sem, recv_sem, device):
        copy = pltpu.make_async_remote_copy(
            src_ref=src, dst_ref=dst, send_sem=send_sem, recv_sem=recv_sem,
            device_id=device, device_id_type=MESH,
        )
        copy.start()
        return copy

    shot_copies, live_copies, tm_copies = {}, {}, []

    def forward(slot, source):
        for side, other in ((0, z_up), (1, z_down)):
            tm_copies.append(
                send(source, blk.at[slot, side], tm_send.at[slot, side], tm_recv.at[slot, side], (s, other))
            )

    for offset in ORDER:
        slot = SLOT[-offset]
        target = (shot_at(offset), z)
        shot_copies[-offset] = send(rec, blk.at[slot, 2], shot_send.at[slot], shot_recv.at[slot], target)
        live_copies[-offset] = send(live, live_in.at[slot], live_send.at[slot], live_recv.at[slot], target)
    forward(0, rec)

    def keep_first(a, near, far):
        c1[a, 0:L, 0:L] = near
        c1[a, 0:L, L:] = far
        c1[a, L:, 0:L] = far
        c1[a, L:, L:] = near

    circulants(des[...], keep_first)

    for offset in ORDER:
        shot_copies[offset].wait_recv()
        forward(SLOT[offset], blk.at[SLOT[offset], 2])

    def keep_second(a, near, far):
        c2[a, 0:L, :] = near
        c2[a, L:, :] = far

    circulants(shp[...], keep_second)

    lane = iota((1, L), 1)
    upper = lane >= CH
    row, col = iota((256, 32), 0), iota((256, 32), 1)
    third = lax.shift_right_logical(col * 43, 7)
    place = (row == GAP * third + (col - 3 * third)) & (col < 6 * SHOT_TAPS)
    first = fw[...]
    doubled = jnp.concatenate([first, first], axis=0)
    b0s[0:16, :] = jnp.zeros((16, L), F32)
    b0s[16:, :] = dot_nt(place.astype(BF)[:, : 6 * SHOT_TAPS], doubled)
    for pair in range(8):
        even, odd = b0s[pl.ds(16 - 2 * pair, 256), :], b0s[pl.ds(15 - 2 * pair, 256), :]
        w0[:, pair * L : (pair + 1) * L] = jnp.where(upper, odd, even).astype(BF)

    same_half = (iota((L, L), 0) >= CH) == (iota((L, L), 1) >= CH)
    zero_block = jnp.zeros((L, L), BF)
    for layer in range(HID):
        weights = hw[layer]
        doubled = jnp.concatenate([weights, weights], axis=0)
        wh[layer, 3 * L :, 0:L] = zero_block
        wh[layer, 0:L, L:] = zero_block
        for k in range(3):
            pick = iota((L, 3 * CH), 1) == (k * CH + (iota((L, 3 * CH), 0) & (CH - 1)))
            block = jnp.where(same_half, dot_nt(pick.astype(BF), doubled), 0.0).astype(BF)
            wh[layer, k * L : (k + 1) * L, 0:L] = block
            wh[layer, (k + 1) * L : (k + 2) * L, L:] = block

    pick = iota((L, CH), 1) == (iota((L, CH), 0) & (CH - 1))
    spread = dot_nt(pick.astype(BF), jnp.broadcast_to(ow[...], (L, CH)))
    for r in range(4):
        for i in range(2):
            step = 8 * i + 2 * r
            here = (iota((L, L), 1) & 15) == step + jnp.where(iota((L, L), 0) >= CH, 1, 0)
            wo[(2 * r + i) * L : (2 * r + i + 1) * L, :] = jnp.where(here, spread, 0.0).astype(BF)

    def wide(bias):
        both = jnp.concatenate([bias, bias], axis=1)
        return jnp.concatenate([both, both], axis=1)

    first_bias = wide(fb[...])
    hidden_bias = [wide(hb[layer : layer + 1, :]) for layer in range(HID)]

    has_left, has_right = z > 0, z < tms - 1
    left_f, right_f = jnp.where(has_left, 1.0, 0.0), jnp.where(has_right, 1.0, 0.0)
    halo = jnp.where(lane < 80, right_f, left_f)
    time_ok = jnp.concatenate([jnp.ones((1, L), F32), halo], axis=1)
    diagonal = iota((N, N), 0) == iota((N, N), 1)

    def live_column(offset):
        values = live[...] if offset == 0 else live_in[SLOT[offset]]
        there = (s + offset >= 0) & (s + offset < shots)
        values = jnp.where(there, values, 0).astype(F32)
        spread_rows = jnp.where(diagonal, jnp.broadcast_to(values, (N, N)), 0.0)
        return jnp.sum(spread_rows, axis=1, keepdims=True)

    kept = {}

    def fill(offset):
        slot = SLOT[offset]
        column = live_column(offset)
        kept[offset] = (column * time_ok) > 0.0
        centre = rec[...] if offset == 0 else blk[slot, 2]
        sides = jnp.where(lane < 80, blk[slot, 1].astype(F32), blk[slot, 0].astype(F32))
        xs[slot, 0:8, :] = jnp.zeros((8, 2 * L), F32)
        xs[slot, 72:80, :] = jnp.zeros((8, 2 * L), F32)
        xs[slot, 8:72, 0:L] = jnp.where(column > 0.0, centre.astype(F32), 0.0)
        xs[slot, 8:72, L:] = jnp.where((column * halo) > 0.0, sides, 0.0)

    def filtered(offsets):
        total = None
        for a in range(FN):
            rows = [xs[SLOT[o], pl.ds(4 + a, N), :] for o in offsets]
            left = jnp.concatenate(rows, axis=0).astype(BF)
            term = dot_nn(left, c1[a])
            total = term if total is None else total + term
        return {o: jnp.where(kept[o], total[i * N : (i + 1) * N], 0.0).astype(BF).astype(F32)
                for i, o in enumerate(offsets)}

    lanes2 = iota((1, 2 * L), 1)

    def make_planes(offset, values):
        a = offset + SHOT_TAPS // 2
        planes[a] = pltpu.roll(values, GAP * a + 33, 1).astype(BF)
        p = a + SHOT_TAPS
        delay = dith[shot_at(offset)]
        moved = pltpu.roll(values, GAP * p + 33 - delay, 1)
        early = (lanes2 >= GAP * p) & (lanes2 < GAP * p + 33)
        planes[p] = jnp.where(jnp.where(early, left_f, 1.0) > 0.0, moved, 0.0).astype(BF)

    own = None
    for offsets in ((0, -1, 1), (-2, 2)):
        for offset in offsets:
            slot = SLOT[offset]
            if offset != 0:
                live_copies[offset].wait_recv()
            for copy in tm_copies[2 * slot : 2 * slot + 2]:
                copy.wait_recv()
            fill(offset)
        done = filtered(offsets)
        for offset in offsets:
            make_planes(offset, done[offset])
        if 0 in done:
            own = done[0]

    for part in range(2):
        rows = slice(part * 32, part * 32 + 32)
        held = [planes[p, rows, :].astype(F32) for p in range(2 * SHOT_TAPS)]
        for g in range(GROUPS):
            place = (lanes2 - 16 * g) & 255
            merged = held[0]
            for p in range(1, 2 * SHOT_TAPS):
                merged = jnp.where(place >= GAP * p, held[p], merged)
            if g:
                merged = pltpu.roll(merged, 256 - 16 * g, 1)
            gs[g, rows, :] = merged.astype(BF)

    def finish(total, bias, factor):
        act = jnp.maximum(total + bias, 0.0)
        if factor is not None:
            act = act * factor
        return act.astype(BF)

    for g0, g1, factor in ((0, 2, left_f), (2, 6, None), (6, 10, None), (10, 12, right_f)):
        left = gs[g0:g1].reshape((g1 - g0) * N, 256)
        for quarter in range(4):
            act = finish(dot_nn(left, w0[:, quarter * 256 : (quarter + 1) * 256]), first_bias, factor)
            for g in range(g0, g1):
                for i in range(2):
                    at = (g - g0) * N
                    a0[8 * g + 2 * quarter + i] = act[at : at + N, i * L : (i + 1) * L]

    def chunks(lo, hi, size):
        cuts = [lo, 16 // size, 80 // size, hi]
        return [(cuts[0], cuts[1], left_f), (cuts[1], cuts[2], None), (cuts[2], cuts[3], right_f)]

    def layer(source, target, index, lo, hi, most):
        step = 1 << index
        for start, stop, factor in chunks(lo, hi, 2 * step):
            for j0 in range(start, stop, most):
                js = range(j0, min(j0 + most, stop))
                us = [2 * step * j + r for j in js for r in range(step)]
                left = jnp.concatenate(
                    [jnp.concatenate([source[u - step], source[u], source[u + step], source[u + 2 * step]], axis=1)
                     for u in us], axis=0)
                act = finish(dot_nn(left, wh[index]), hidden_bias[index], factor)
                target(us, step, act)

    def into(ref):
        def keep(us, step, act):
            for m, u in enumerate(us):
                ref[u] = act[m * N : (m + 1) * N, 0:L]
                ref[u + step] = act[m * N : (m + 1) * N, L:]
        return keep

    column = live_column(0)
    alive = column > 0.0
    out_bias = ob[0]
    sixteen = lax.shift_right_logical(lane, 4)
    pred = {}

    def finish_pred(us, step, act):
        for q in range(len(us) // step):
            left = jnp.concatenate(
                [act[(q * step + r) * N : (q * step + r + 1) * N] for r in range(step)], axis=1)
            pred[us[q * step] // 8] = (dot_nn(left, wo[...]) + out_bias).astype(BF).astype(F32)

    layer(a0, into(a1), 0, 1, 47, 8)
    layer(a1, into(a2), 1, 1, 23, 4)
    layer(a2, finish_pred, 2, 1, 11, 2)

    middle = pred[2]
    for j in range(3, 10):
        middle = jnp.where(sixteen == j - 2, pred[j], middle)
    middle = jnp.where(alive, middle, 0.0)
    inter_out[...] = middle.astype(BF)
    edge = jnp.where(lane < 80, pred[10], pred[1])
    edge = jnp.where((column * halo) > 0.0, edge, 0.0)
    rest = (own - jnp.concatenate([middle, edge], axis=1)).astype(BF).astype(F32)
    ds[0:8, :] = jnp.zeros((8, 2 * L), F32)
    ds[72:80, :] = jnp.zeros((8, 2 * L), F32)
    ds[8:72, :] = rest
    total = None
    for a in range(FN):
        term = dot_nn(ds[pl.ds(4 + a, N), :].astype(BF), c2[a])
        total = term if total is None else total + term
    clean_out[...] = jnp.where(alive, total, 0.0).astype(BF)

    for copy in list(shot_copies.values()) + list(live_copies.values()) + tm_copies:
        copy.wait_send()


def local(shots, tms, records, live, dither, designature, first_weights, first_bias, hidden_weights, hidden_bias,
          out_weights, out_bias, shaping):
    vmem = pl.BlockSpec(memory_space=pltpu.VMEM)
    smem = pl.BlockSpec(memory_space=pltpu.SMEM)
    shape = jax.ShapeDtypeStruct((N, L), BF)
    inter, clean = pl.pallas_call(
        functools.partial(kernel, shots, tms),
        out_shape=(shape, shape),
        in_specs=[vmem, vmem, smem, vmem, vmem, vmem, vmem, vmem, vmem, smem, vmem],
        out_specs=(vmem, vmem),
        scratch_shapes=[
            pltpu.VMEM((5, 3, N, L), BF),
            pltpu.VMEM((5, 1, N), jnp.int32),
            pltpu.VMEM((5, 80, 2 * L), F32),
            pltpu.VMEM((FN, 2 * L, 2 * L), BF),
            pltpu.VMEM((FN, 2 * L, L), BF),
            pltpu.VMEM((256, 1024), BF),
            pltpu.VMEM((HID, 4 * L, 2 * L), BF),
            pltpu.VMEM((1024, L), BF),
            pltpu.VMEM((272, L), F32),
            pltpu.VMEM((2 * SHOT_TAPS, N, 2 * L), BF),
            pltpu.VMEM((GROUPS, N, 2 * L), BF),
            pltpu.VMEM((US, N, L), BF),
            pltpu.VMEM((US, N, L), BF),
            pltpu.VMEM((US, N, L), BF),
            pltpu.VMEM((80, 2 * L), F32),
            pltpu.SemaphoreType.DMA((5,)),
            pltpu.SemaphoreType.DMA((5,)),
            pltpu.SemaphoreType.DMA((5,)),
            pltpu.SemaphoreType.DMA((5,)),
            pltpu.SemaphoreType.DMA((5, 2)),
            pltpu.SemaphoreType.DMA((5, 2)),
        ],
        compiler_params=pltpu.CompilerParams(
            collective_id=0, has_side_effects=True, vmem_limit_bytes=48 * 1024 * 1024
        ),
    )(
        records.reshape(N, L),
        live,
        dither,
        designature,
        first_weights,
        first_bias.reshape(1, CH),
        hidden_weights,
        hidden_bias,
        out_weights.reshape(1, CH),
        out_bias,
        shaping,
    )
    return inter.reshape(1, N, L), clean.reshape(1, N, L)


def solution(mesh):
    shots, tms = mesh.shape["shot"], mesh.shape["tm"]
    in_specs = (P("shot", None, "tm"), P("shot", None), P(), P(), P(), P(), P(), P(), P(), P(), P())
    out_specs = (P("shot", None, "tm"), P("shot", None, "tm"))
    return jax.shard_map(
        functools.partial(local, shots, tms), mesh=mesh, in_specs=in_specs, out_specs=out_specs, check_vma=False
    )
```

time: 79.5 us -> 30.5 us (0.38)
  the two profiles are of different devices: /device:TPU:225 before, /device:TPU:1 now
where the time goes in v1:
time: 30.5 us; the launch traced here: 30.3 us
  Pallas kernels  25.9 us (85%)
  local copies, waits for them, and re-layouts  2.97 us (10%)
  between operations  1.43 us (5%)
    pallas_call x1, Pallas kernels, local(): pl.pallas_call(functools.partial(kernel, shots, tms), out_shape=(shape, s...  25.9 us
    unnamed x21, local copies, waits for them, and re-layouts  2.97 us

profile of v1, /device:TPU:1, one launch (start us, length us, event | category | flops | bytes accessed | tf_op | source)
XLA Modules:
  0.0 30.3 jit_solution(9024737152294124239)
XLA Ops:
  0.6 0.0 copy-start.1
  1.3 0.0 copy-start.2
  1.3 0.0 copy-start.3
  1.3 0.0 copy-start.4
  1.3 0.0 copy-start.5
  1.3 0.0 copy-start.6
  1.4 0.0 copy-start.7
  1.4 0.0 copy-start.8
  1.4 0.8 %copy.13.fw = bf16[64,30]{1,0:T(8,128)(2,1)S(1)} copy(bf16[64,30]{0,1:T(8,128)(2,1)} %param.15) | data formatting | bytes 7680 | tf_op args[4]
  2.2 0.0 copy-done.1
  2.2 0.0 copy-done.2
  2.2 0.0 copy-done.3
  2.2 0.0 copy-done.4
  2.2 0.0 copy-done.5
  2.2 0.0 copy-done.6
  2.3 0.0 copy-done.7
  2.3 0.0 copy-done.8
  2.3 0.0 copy-start
  2.3 0.9 %copy-done = bf16[3,64,192]{2,1,0:T(8,128)(2,1)S(1)} copy-done((bf16[3,64,192]{2,1,0:T(8,128)(2,1)S(1)}, bf16[3,64,192]{2,1,0:T(8,128)(2,1)}, u32[]{:S(2)}) %copy-start) | copy-done | bytes 73752
  3.2 25.9 %shard_map.122 = (bf16[64,128]{1,0:T(8,128)(2,1)S(1)}, bf16[64,128]{1,0:T(8,128)(2,1)S(1)}) custom-call(bf16[64,128]{1,0:T(8,128)(2,1)S(1)} %bitcast.5, s32[1,64]{1,0:T(1,128)S(1)} %copy-done.5, s32[32]{0:T(128)S(1)} %copy-done.6, bf16[9,33]{1,0:T(8,128)(2,1)S(1)} %copy-done.2, bf16[64,30]{1,0:T(8,128)(2,1)S(1)} %copy.13.fw, f32[1,64]{1,0:T(1,128)S(1)} %bitcast.8, ...), custom_call_target="tpu_custom_call" | custom-call | tf_op jit(solution)/shard_map/pallas_call | solution.py:336
  29.1 0.6 %copy.17 = bf16[1,64,128]{2,1,0:T(8,128)(2,1)} copy(bf16[1,64,128]{2,1,0:T(8,128)(2,1)S(1)} %bitcast.7) | data formatting | bytes 32768
  29.7 0.6 %copy.18 = bf16[1,64,128]{2,1,0:T(8,128)(2,1)} copy(bf16[1,64,128]{2,1,0:T(8,128)(2,1)S(1)} %bitcast.6) | data formatting | bytes 32768
Async XLA Ops:
  0.6 1.6 %copy-start.1 = (bf16[1,64,128]{2,1,0:T(8,128)(2,1)S(1)}, bf16[1,64,128]{2,1,0:T(8,128)(2,1)}, u32[]{:S(2)}) copy-start(bf16[1,64,128]{2,1,0:T(8,128)(2,1)} %param.11) | copy-start | bytes 49156
  1.3 0.9 %copy-start.2 = (bf16[9,33]{1,0:T(8,128)(2,1)S(1)}, bf16[9,33]{1,0:T(8,128)(2,1)}, u32[]{:S(2)}) copy-start(bf16[9,33]{1,0:T(8,128)(2,1)} %des.1) | copy-start | bytes 1786
  1.3 0.9 %copy-start.3 = (bf16[9,33]{1,0:T(8,128)(2,1)S(1)}, bf16[9,33]{1,0:T(8,128)(2,1)}, u32[]{:S(2)}) copy-start(bf16[9,33]{1,0:T(8,128)(2,1)} %shp.1) | copy-start | bytes 1786
  1.3 0.9 %copy-start.4 = (f32[3,64]{1,0:T(4,128)S(1)}, f32[3,64]{1,0:T(4,128)}, u32[]{:S(2)}) copy-start(f32[3,64]{1,0:T(4,128)} %hb.1) | copy-start | bytes 2308
  1.3 0.9 %copy-start.5 = (s32[1,64]{1,0:T(1,128)S(1)}, s32[1,64]{1,0:T(1,128)}, u32[]{:S(2)}) copy-start(s32[1,64]{1,0:T(1,128)} %live.1) | copy-start | bytes 772
  1.3 0.9 %copy-start.6 = (s32[32]{0:T(128)S(1)}, s32[32]{0:T(128)}, u32[]{:S(2)}) copy-start(s32[32]{0:T(128)} %dith.1) | copy-start | bytes 388
  1.4 0.9 %copy-start.7 = (f32[64]{0:T(128)S(1)}, f32[64]{0:T(128)}, u32[]{:S(2)}) copy-start(f32[64]{0:T(128)} %param.16) | copy-start | bytes 772
  1.4 0.9 %copy-start.8 = (bf16[64]{0:T(256)(128)(2,1)S(1)}, bf16[64]{0:T(256)(128)(2,1)}, u32[]{:S(2)}) copy-start(bf16[64]{0:T(256)(128)(2,1)} %param.19) | copy-start | bytes 388
  2.3 0.9 %copy-start = (bf16[3,64,192]{2,1,0:T(8,128)(2,1)S(1)}, bf16[3,64,192]{2,1,0:T(8,128)(2,1)}, u32[]{:S(2)}) copy-start(bf16[3,64,192]{2,1,0:T(8,128)(2,1)} %hw.1) | copy-start | bytes 221188

commit v2 on v1

v2 whole, which is shorter than its diff:
```python
import functools

import jax
import jax.numpy as jnp
from jax import lax
from jax.experimental import pallas as pl
from jax.experimental.pallas import tpu as pltpu
from jax.sharding import PartitionSpec as P

HID = 3
FN = 9
FT = 33
SHOT_TAPS = 5
CH = 64
N = 64
L = 128
GAP = 24
GROUPS = 12
US = 8 * GROUPS
SLOT = {0: 0, -1: 1, 1: 2, -2: 3, 2: 4}
MESH = pl.DeviceIdType.MESH
BF = jnp.bfloat16
F32 = jnp.float32


def iota(shape, dim):
    return lax.broadcasted_iota(jnp.int32, shape, dim)


def dot_nn(a, b):
    return jnp.dot(a, b, preferred_element_type=F32)


def dot_nt(a, b):
    return lax.dot_general(a, b, (((1,), (1,)), ((), ())), preferred_element_type=F32)


def circulants(taps, store):
    pick = iota((FT, L), 0) == ((FT // 2 - iota((FT, L), 1)) & (L - 1))
    rows = dot_nn(taps, pick.astype(BF))
    near = jnp.abs(iota((L, L), 0) - iota((L, L), 1)) <= L // 2
    for a in range(FN):
        full = jnp.broadcast_to(rows[a : a + 1, :], (L, L))
        full = pltpu.roll(full, 0, 1, stride=1, stride_axis=0)
        store(a, jnp.where(near, full, 0.0).astype(BF), jnp.where(near, 0.0, full).astype(BF))


def kernel(
    shots,
    tms,
    rec_hbm,
    live_hbm,
    dith_hbm,
    des_hbm,
    fw_hbm,
    fb_hbm,
    hw_hbm,
    hb_hbm,
    ow_hbm,
    ob_hbm,
    shp_hbm,
    inter_out,
    clean_out,
    rec,
    live,
    dith,
    des,
    fw,
    fb,
    hw,
    hb,
    ow,
    ob,
    shp,
    halos,
    win,
    xs,
    c1,
    c2,
    w0,
    wh,
    wo,
    b0s,
    planes,
    gs,
    a0,
    a1,
    a2,
    ds,
    in_sem,
    tm_send,
    tm_recv,
    shot_send,
    shot_recv,
):
    s, z = lax.axis_index("shot"), lax.axis_index("tm")
    has_left, has_right = z > 0, z < tms - 1
    has_before, has_after = s > 0, s < shots - 1
    has_before2, has_after2 = s > 1, s < shots - 2

    barrier = pltpu.get_barrier_semaphore()
    expected = 0
    for here, device in (
        (has_left, (s, z - 1)),
        (has_right, (s, z + 1)),
        (has_before, (s - 1, z)),
        (has_after, (s + 1, z)),
    ):
        @pl.when(here)
        def _(device=device):
            pl.semaphore_signal(barrier, inc=1, device_id=device, device_id_type=MESH)
        expected = expected + here.astype(jnp.int32)

    fetches = [
        pltpu.make_async_copy(src, dst, in_sem.at[i])
        for i, (src, dst) in enumerate((
            (des_hbm, des), (rec_hbm, rec), (live_hbm, live), (fw_hbm, fw), (hw_hbm, hw), (dith_hbm, dith),
            (ow_hbm, ow), (shp_hbm, shp), (fb_hbm, fb), (hb_hbm, hb), (ob_hbm, ob)))
    ]
    for fetch in fetches:
        fetch.start()

    def remote(src, dst, send_sem, recv_sem, device):
        return pltpu.make_async_remote_copy(
            src_ref=src, dst_ref=dst, send_sem=send_sem, recv_sem=recv_sem,
            device_id=device, device_id_type=MESH,
        )

    to_right = remote(rec_hbm, halos.at[0], tm_send.at[0], tm_recv.at[0], (s, z + 1))
    to_left = remote(rec_hbm, halos.at[1], tm_send.at[1], tm_recv.at[1], (s, z - 1))

    def to_shot(index, source, target, device):
        return remote(win.at[SLOT[source]], win.at[SLOT[target]], shot_send.at[index], shot_recv.at[index], device)

    to_after = to_shot(0, 0, -1, (s + 1, z))
    to_before = to_shot(1, 0, 1, (s - 1, z))
    on_after = to_shot(2, -1, -2, (s + 1, z))
    on_before = to_shot(3, 1, 2, (s - 1, z))

    def keep_first(a, near, far):
        c1[a, 0:L, 0:L] = near
        c1[a, 0:L, L:] = far
        c1[a, L:, 0:L] = far
        c1[a, L:, L:] = near

    fetches[0].wait()
    circulants(des[...], keep_first)

    pl.semaphore_wait(barrier, expected)

    @pl.when(has_right)
    def _():
        to_right.start()

    @pl.when(has_left)
    def _():
        to_left.start()

    for fetch in fetches[1:]:
        fetch.wait()

    lane = iota((1, L), 1)
    left_f, right_f = jnp.where(has_left, 1.0, 0.0), jnp.where(has_right, 1.0, 0.0)
    halo = jnp.where(lane < 80, right_f, left_f)
    time_ok = jnp.concatenate([jnp.ones((1, L), F32), halo], axis=1)
    diagonal = iota((N, N), 0) == iota((N, N), 1)
    spread_rows = jnp.where(diagonal, jnp.broadcast_to(live[...].astype(F32), (N, N)), 0.0)
    column = jnp.sum(spread_rows, axis=1, keepdims=True)
    alive = column > 0.0
    alive_halo = (column * halo) > 0.0

    xs[0:8, :] = jnp.zeros((8, 2 * L), F32)
    xs[72:80, :] = jnp.zeros((8, 2 * L), F32)
    xs[8:72, 0:L] = jnp.where(alive, rec[...].astype(F32), 0.0)

    upper = lane >= CH
    row, col = iota((256, 6 * SHOT_TAPS), 0), iota((256, 6 * SHOT_TAPS), 1)
    third = lax.shift_right_logical(col * 43, 7)
    place = row == GAP * third + (col - 3 * third)
    base = dot_nn(place.astype(BF), fw[...])
    b0s[0:16, :] = jnp.zeros((16, L), F32)
    b0s[16:, :] = jnp.concatenate([base, base], axis=1)
    for pair in range(8):
        even, odd = b0s[pl.ds(16 - 2 * pair, 256), :], b0s[pl.ds(15 - 2 * pair, 256), :]
        w0[:, pair * L : (pair + 1) * L] = jnp.where(upper, odd, even).astype(BF)

    @pl.when(has_left)
    def _():
        to_right.wait_recv()

    @pl.when(has_right)
    def _():
        to_left.wait_recv()

    sides = jnp.where(lane < 80, halos[1].astype(F32), halos[0].astype(F32))
    xs[8:72, L:] = jnp.where(alive_halo, sides, 0.0)

    def filter_with(source, matrices):
        total = None
        for a in range(FN):
            term = dot_nn(source[pl.ds(4 + a, N), :].astype(BF), matrices[a])
            total = term if total is None else total + term
        return total

    win[0] = jnp.where((column * time_ok) > 0.0, filter_with(xs, c1), 0.0).astype(BF)

    @pl.when(has_after)
    def _():
        to_after.start()

    @pl.when(has_before)
    def _():
        to_before.start()

    lanes2 = iota((1, 2 * L), 1)

    def make_planes(offset, there):
        values = win[SLOT[offset]].astype(F32)
        if there is not None:
            values = jnp.where(there, values, 0.0)
        a = offset + SHOT_TAPS // 2
        planes[a] = pltpu.roll(values, GAP * a + 33, 1).astype(BF)
        p = a + SHOT_TAPS
        delay = dith[lax.rem(s + offset + shots, shots)]
        moved = pltpu.roll(values, GAP * p + 33 - delay, 1)
        early = (lanes2 >= GAP * p) & (lanes2 < GAP * p + 33)
        planes[p] = jnp.where(jnp.where(early, left_f, 1.0) > 0.0, moved, 0.0).astype(BF)

    same_half = (iota((L, L), 0) >= CH) == (iota((L, L), 1) >= CH)
    zero_block = jnp.zeros((L, L), BF)
    for layer in range(HID):
        weights = hw[layer]
        doubled = jnp.concatenate([weights, weights], axis=0)
        wh[layer, 3 * L :, 0:L] = zero_block
        wh[layer, 0:L, L:] = zero_block
        for k in range(3):
            pick = iota((L, 3 * CH), 1) == (k * CH + (iota((L, 3 * CH), 0) & (CH - 1)))
            block = jnp.where(same_half, dot_nt(pick.astype(BF), doubled), 0.0).astype(BF)
            wh[layer, k * L : (k + 1) * L, 0:L] = block
            wh[layer, (k + 1) * L : (k + 2) * L, L:] = block

    pick = iota((L, CH), 1) == (iota((L, CH), 0) & (CH - 1))
    spread = dot_nt(pick.astype(BF), jnp.broadcast_to(ow[...], (L, CH)))
    for r in range(4):
        for i in range(2):
            step = 8 * i + 2 * r
            here = (iota((L, L), 1) & 15) == step + jnp.where(iota((L, L), 0) >= CH, 1, 0)
            wo[(2 * r + i) * L : (2 * r + i + 1) * L, :] = jnp.where(here, spread, 0.0).astype(BF)

    def wide(bias):
        both = jnp.concatenate([bias, bias], axis=1)
        return jnp.concatenate([both, both], axis=1)

    first_bias = wide(fb[...])
    hidden_bias = [wide(hb[layer : layer + 1, :]) for layer in range(HID)]
    make_planes(0, None)

    @pl.when(has_before)
    def _():
        to_after.wait_recv()

    @pl.when(has_before & has_after)
    def _():
        on_after.start()

    @pl.when(has_after)
    def _():
        to_before.wait_recv()

    @pl.when(has_before & has_after)
    def _():
        on_before.start()

    def keep_second(a, near, far):
        c2[a, 0:L, :] = near
        c2[a, L:, :] = far

    circulants(shp[...], keep_second)
    make_planes(-1, has_before)
    make_planes(1, has_after)

    @pl.when(has_before2)
    def _():
        on_after.wait_recv()

    @pl.when(has_after2)
    def _():
        on_before.wait_recv()

    make_planes(-2, has_before2)
    make_planes(2, has_after2)

    for part in range(2):
        rows = slice(part * 32, part * 32 + 32)
        held = [planes[p, rows, :].astype(F32) for p in range(2 * SHOT_TAPS)]
        for g in range(GROUPS):
            place = (lanes2 - 16 * g) & 255
            merged = held[0]
            for p in range(1, 2 * SHOT_TAPS):
                merged = jnp.where(place >= GAP * p, held[p], merged)
            if g:
                merged = pltpu.roll(merged, 256 - 16 * g, 1)
            gs[g, rows, :] = merged.astype(BF)

    def finish(total, bias, factor):
        act = jnp.maximum(total + bias, 0.0)
        if factor is not None:
            act = act * factor
        return act.astype(BF)

    for g0, g1, factor in ((0, 2, left_f), (2, 6, None), (6, 10, None), (10, 12, right_f)):
        left = gs[g0:g1].reshape((g1 - g0) * N, 256)
        for quarter in range(4):
            act = finish(dot_nn(left, w0[:, quarter * 256 : (quarter + 1) * 256]), first_bias, factor)
            for g in range(g0, g1):
                for i in range(2):
                    at = (g - g0) * N
                    a0[8 * g + 2 * quarter + i] = act[at : at + N, i * L : (i + 1) * L]

    def chunks(lo, hi, size):
        cuts = [lo, 16 // size, 80 // size, hi]
        return [(cuts[0], cuts[1], left_f), (cuts[1], cuts[2], None), (cuts[2], cuts[3], right_f)]

    def layer(source, target, index, lo, hi, most):
        step = 1 << index
        for start, stop, factor in chunks(lo, hi, 2 * step):
            for j0 in range(start, stop, most):
                js = range(j0, min(j0 + most, stop))
                us = [2 * step * j + r for j in js for r in range(step)]
                left = jnp.concatenate(
                    [jnp.concatenate([source[u - step], source[u], source[u + step], source[u + 2 * step]], axis=1)
                     for u in us], axis=0)
                act = finish(dot_nn(left, wh[index]), hidden_bias[index], factor)
                target(us, step, act)

    def into(ref):
        def keep(us, step, act):
            for m, u in enumerate(us):
                ref[u] = act[m * N : (m + 1) * N, 0:L]
                ref[u + step] = act[m * N : (m + 1) * N, L:]
        return keep

    out_bias = ob[0]
    sixteen = lax.shift_right_logical(lane, 4)
    pred = {}

    def finish_pred(us, step, act):
        for q in range(len(us) // step):
            left = jnp.concatenate(
                [act[(q * step + r) * N : (q * step + r + 1) * N] for r in range(step)], axis=1)
            pred[us[q * step] // 8] = (dot_nn(left, wo[...]) + out_bias).astype(BF).astype(F32)

    layer(a0, into(a1), 0, 1, 47, 8)
    layer(a1, into(a2), 1, 1, 23, 4)
    layer(a2, finish_pred, 2, 1, 11, 2)

    middle = pred[2]
    for j in range(3, 10):
        middle = jnp.where(sixteen == j - 2, pred[j], middle)
    middle = jnp.where(alive, middle, 0.0)
    inter_out[...] = middle.astype(BF)
    edge = jnp.where(lane < 80, pred[10], pred[1])
    edge = jnp.where(alive_halo, edge, 0.0)
    rest = (win[0].astype(F32) - jnp.concatenate([middle, edge], axis=1)).astype(BF).astype(F32)
    ds[0:8, :] = jnp.zeros((8, 2 * L), F32)
    ds[72:80, :] = jnp.zeros((8, 2 * L), F32)
    ds[8:72, :] = rest
    clean_out[...] = jnp.where(alive, filter_with(ds, c2), 0.0).astype(BF)

    for here, copy in (
        (has_right, to_right),
        (has_left, to_left),
        (has_after, to_after),
        (has_before, to_before),
        (has_before & has_after, on_after),
        (has_before & has_after, on_before),
    ):
        @pl.when(here)
        def _(copy=copy):
            copy.wait_send()


def local(shots, tms, records, live, dither, designature, first_weights, first_bias, hidden_weights, hidden_bias,
          out_weights, out_bias, shaping):
    vmem = pl.BlockSpec(memory_space=pltpu.VMEM)
    hbm = pl.BlockSpec(memory_space=pltpu.HBM)
    shape = jax.ShapeDtypeStruct((N, L), BF)
    inputs = (
        records.reshape(N, L),
        live,
        dither,
        designature,
        first_weights.T,
        first_bias.reshape(1, CH),
        hidden_weights,
        hidden_bias,
        out_weights.reshape(1, CH),
        out_bias,
        shaping,
    )
    spaces = [pltpu.SMEM if i in (2, 9) else pltpu.VMEM for i in range(len(inputs))]
    inter, clean = pl.pallas_call(
        functools.partial(kernel, shots, tms),
        out_shape=(shape, shape),
        in_specs=[hbm] * len(inputs),
        out_specs=(vmem, vmem),
        scratch_shapes=[
            *[space(x.shape, x.dtype) for space, x in zip(spaces, inputs)],
            pltpu.VMEM((2, N, L), BF),
            pltpu.VMEM((5, N, 2 * L), BF),
            pltpu.VMEM((80, 2 * L), F32),
            pltpu.VMEM((FN, 2 * L, 2 * L), BF),
            pltpu.VMEM((FN, 2 * L, L), BF),
            pltpu.VMEM((256, 1024), BF),
            pltpu.VMEM((HID, 4 * L, 2 * L), BF),
            pltpu.VMEM((1024, L), BF),
            pltpu.VMEM((272, L), F32),
            pltpu.VMEM((2 * SHOT_TAPS, N, 2 * L), BF),
            pltpu.VMEM((GROUPS, N, 2 * L), BF),
            pltpu.VMEM((US, N, L), BF),
            pltpu.VMEM((US, N, L), BF),
            pltpu.VMEM((US, N, L), BF),
            pltpu.VMEM((80, 2 * L), F32),
            pltpu.SemaphoreType.DMA((len(inputs),)),
            pltpu.SemaphoreType.DMA((2,)),
            pltpu.SemaphoreType.DMA((2,)),
            pltpu.SemaphoreType.DMA((4,)),
            pltpu.SemaphoreType.DMA((4,)),
        ],
        compiler_params=pltpu.CompilerParams(
            collective_id=0, has_side_effects=True, vmem_limit_bytes=61 * 1024 * 1024
        ),
    )(*inputs)
    return inter.reshape(1, N, L), clean.reshape(1, N, L)


def solution(mesh):
    shots, tms = mesh.shape["shot"], mesh.shape["tm"]
    in_specs = (P("shot", None, "tm"), P("shot", None), P(), P(), P(), P(), P(), P(), P(), P(), P())
    out_specs = (P("shot", None, "tm"), P("shot", None, "tm"))
    return jax.shard_map(
        functools.partial(local, shots, tms), mesh=mesh, in_specs=in_specs, out_specs=out_specs, check_vma=False
    )
```

time: 30.5 us -> 26.4 us (0.87)
  the two profiles are of different devices: /device:TPU:1 before, /device:TPU:223 now
where the time goes in v2:
time: 26.4 us; the launch traced here: 26.2 us
  Pallas kernels  23 us (87%)
  local copies, waits for them, and re-layouts  1.94 us (7%)
  between operations  1.3 us (5%)
    pallas_call x1, Pallas kernels, local(): pl.pallas_call(functools.partial(kernel, shots, tms), out_shape=(shape, s...  23 us
    unnamed x4, local copies, waits for them, and re-layouts  1.94 us

profile of v2, /device:TPU:223, one launch (start us, length us, event | category | flops | bytes accessed | tf_op | source)
XLA Modules:
  0.0 26.2 jit_solution(5957420649293374134)
XLA Ops:
  1.3 23.0 %shard_map.122 = (bf16[64,128]{1,0:T(8,128)(2,1)}, bf16[64,128]{1,0:T(8,128)(2,1)}) custom-call(bf16[64,128]{1,0:T(8,128)(2,1)} %bitcast.6, s32[1,64]{1,0:T(1,128)} %live_hbm.1, s32[32]{0:T(128)} %dith_hbm.1, bf16[9,33]{1,0:T(8,128)(2,1)} %des_hbm.1, bf16[30,64]{1,0:T(8,128)(2,1)} %bitcast.9, f32[1,64]{1,0:T(1,128)} %bitcast.10, bf16[3,64,192]{2,1,0:T(8,128)(2,1)} %hw_hbm.1, ...), custom_call_target="tpu_custom_call" | custom-call | tf_op jit(solution)/shard_map/pallas_call | solution.py:402
  24.3 0.0 copy-start
  24.3 1.3 %copy.16 = bf16[1,64,128]{2,1,0:T(8,128)(2,1)} copy(bf16[1,64,128]{2,1,0:T(8,128)(2,1)} %bitcast.8) | data formatting | bytes 32768
  25.6 0.0 copy-done
  25.6 0.6 %copy.17 = bf16[1,64,128]{2,1,0:T(8,128)(2,1)} copy(bf16[1,64,128]{2,1,0:T(8,128)(2,1)S(1)} %bitcast.7) | data formatting | bytes 32768
Async XLA Ops:
  24.3 1.3 %copy-start = (bf16[64,128]{1,0:T(8,128)(2,1)S(1)}, bf16[64,128]{1,0:T(8,128)(2,1)}, u32[]{:S(2)}) copy-start(bf16[64,128]{1,0:T(8,128)(2,1)} %get-tuple-element.5) | copy-start | bytes 49156

commit v3 on v2

--- a/solution.py
+++ b/solution.py
@@ -59,8 +59,7 @@
     ow_hbm,
     ob_hbm,
     shp_hbm,
-    inter_out,
-    clean_out,
+    out,
     rec,
     live,
     dith,
@@ -86,6 +85,7 @@
     a0,
     a1,
     a2,
+    a3,
     ds,
     in_sem,
     tm_send,
@@ -105,6 +105,8 @@
         (has_right, (s, z + 1)),
         (has_before, (s - 1, z)),
         (has_after, (s + 1, z)),
+        (has_before2, (s - 2, z)),
+        (has_after2, (s + 2, z)),
     ):
         @pl.when(here)
         def _(device=device):
@@ -129,13 +131,18 @@
     to_right = remote(rec_hbm, halos.at[0], tm_send.at[0], tm_recv.at[0], (s, z + 1))
     to_left = remote(rec_hbm, halos.at[1], tm_send.at[1], tm_recv.at[1], (s, z - 1))
 
-    def to_shot(index, source, target, device):
-        return remote(win.at[SLOT[source]], win.at[SLOT[target]], shot_send.at[index], shot_recv.at[index], device)
-
-    to_after = to_shot(0, 0, -1, (s + 1, z))
-    to_before = to_shot(1, 0, 1, (s - 1, z))
-    on_after = to_shot(2, -1, -2, (s + 1, z))
-    on_before = to_shot(3, 1, 2, (s - 1, z))
+    def to_shot(index, offset):
+        return remote(
+            win.at[0], win.at[SLOT[-offset]], shot_send.at[index], shot_recv.at[index], (s + offset, z))
+
+    shot_copies = [
+        (to_shot(i, offset), there, behind)
+        for i, (offset, there, behind) in enumerate((
+            (2, has_after2, has_before2),
+            (-2, has_before2, has_after2),
+            (1, has_after, has_before),
+            (-1, has_before, has_after)))
+    ]
 
     def keep_first(a, near, far):
         c1[a, 0:L, 0:L] = near
@@ -204,13 +211,10 @@
 
     win[0] = jnp.where((column * time_ok) > 0.0, filter_with(xs, c1), 0.0).astype(BF)
 
-    @pl.when(has_after)
-    def _():
-        to_after.start()
-
-    @pl.when(has_before)
-    def _():
-        to_before.start()
+    for copy, there, _ in shot_copies:
+        @pl.when(there)
+        def _(copy=copy):
+            copy.start()
 
     lanes2 = iota((1, 2 * L), 1)
 
@@ -255,40 +259,18 @@
     hidden_bias = [wide(hb[layer : layer + 1, :]) for layer in range(HID)]
     make_planes(0, None)
 
-    @pl.when(has_before)
-    def _():
-        to_after.wait_recv()
-
-    @pl.when(has_before & has_after)
-    def _():
-        on_after.start()
-
-    @pl.when(has_after)
-    def _():
-        to_before.wait_recv()
-
-    @pl.when(has_before & has_after)
-    def _():
-        on_before.start()
-
     def keep_second(a, near, far):
         c2[a, 0:L, :] = near
         c2[a, L:, :] = far
 
     circulants(shp[...], keep_second)
-    make_planes(-1, has_before)
-    make_planes(1, has_after)
-
-    @pl.when(has_before2)
-    def _():
-        on_after.wait_recv()
-
-    @pl.when(has_after2)
-    def _():
-        on_before.wait_recv()
-
-    make_planes(-2, has_before2)
-    make_planes(2, has_after2)
+    for i, offset in ((2, -1), (3, 1), (0, -2), (1, 2)):
+        copy, _, behind = shot_copies[i]
+
+        @pl.when(behind)
+        def _(copy=copy):
+            copy.wait_recv()
+        make_planes(offset, behind)
 
     for part in range(2):
         rows = slice(part * 32, part * 32 + 32)
@@ -342,38 +324,35 @@
 
     out_bias = ob[0]
     sixteen = lax.shift_right_logical(lane, 4)
-    pred = {}
-
-    def finish_pred(us, step, act):
-        for q in range(len(us) // step):
-            left = jnp.concatenate(
-                [act[(q * step + r) * N : (q * step + r + 1) * N] for r in range(step)], axis=1)
-            pred[us[q * step] // 8] = (dot_nn(left, wo[...]) + out_bias).astype(BF).astype(F32)
+
+    def last(us, step, act):
+        for m, u in enumerate(us):
+            r = m % step
+            a3[u // 8 - 1, :, 2 * L * r : 2 * L * (r + 1)] = act[m * N : (m + 1) * N]
 
     layer(a0, into(a1), 0, 1, 47, 8)
     layer(a1, into(a2), 1, 1, 23, 4)
-    layer(a2, finish_pred, 2, 1, 11, 2)
+    layer(a2, last, 2, 1, 11, 2)
+    scores = (dot_nn(a3[...].reshape(10 * N, 8 * L), wo[...]) + out_bias).astype(BF).astype(F32)
+    pred = {j: scores[(j - 1) * N : j * N] for j in range(1, 11)}
 
     middle = pred[2]
     for j in range(3, 10):
         middle = jnp.where(sixteen == j - 2, pred[j], middle)
     middle = jnp.where(alive, middle, 0.0)
-    inter_out[...] = middle.astype(BF)
+    out[0] = middle.astype(BF)
     edge = jnp.where(lane < 80, pred[10], pred[1])
     edge = jnp.where(alive_halo, edge, 0.0)
     rest = (win[0].astype(F32) - jnp.concatenate([middle, edge], axis=1)).astype(BF).astype(F32)
     ds[0:8, :] = jnp.zeros((8, 2 * L), F32)
     ds[72:80, :] = jnp.zeros((8, 2 * L), F32)
     ds[8:72, :] = rest
-    clean_out[...] = jnp.where(alive, filter_with(ds, c2), 0.0).astype(BF)
+    out[1] = jnp.where(alive, filter_with(ds, c2), 0.0).astype(BF)
 
     for here, copy in (
         (has_right, to_right),
         (has_left, to_left),
-        (has_after, to_after),
-        (has_before, to_before),
-        (has_before & has_after, on_after),
-        (has_before & has_after, on_before),
+        *[(there, copy) for copy, there, _ in shot_copies],
     ):
         @pl.when(here)
         def _(copy=copy):
@@ -384,7 +363,7 @@
           out_weights, out_bias, shaping):
     vmem = pl.BlockSpec(memory_space=pltpu.VMEM)
     hbm = pl.BlockSpec(memory_space=pltpu.HBM)
-    shape = jax.ShapeDtypeStruct((N, L), BF)
+    shape = pltpu.VMEM((2, N, L), BF)
     inputs = (
         records.reshape(N, L),
         live,
@@ -399,11 +378,11 @@
         shaping,
     )
     spaces = [pltpu.SMEM if i in (2, 9) else pltpu.VMEM for i in range(len(inputs))]
-    inter, clean = pl.pallas_call(
+    both = pl.pallas_call(
         functools.partial(kernel, shots, tms),
-        out_shape=(shape, shape),
+        out_shape=shape,
         in_specs=[hbm] * len(inputs),
-        out_specs=(vmem, vmem),
+        out_specs=vmem,
         scratch_shapes=[
             *[space(x.shape, x.dtype) for space, x in zip(spaces, inputs)],
             pltpu.VMEM((2, N, L), BF),
@@ -420,6 +399,7 @@
             pltpu.VMEM((US, N, L), BF),
             pltpu.VMEM((US, N, L), BF),
             pltpu.VMEM((US, N, L), BF),
+            pltpu.VMEM((10, N, 8 * L), BF),
             pltpu.VMEM((80, 2 * L), F32),
             pltpu.SemaphoreType.DMA((len(inputs),)),
             pltpu.SemaphoreType.DMA((2,)),
@@ -431,7 +411,7 @@
             collective_id=0, has_side_effects=True, vmem_limit_bytes=61 * 1024 * 1024
         ),
     )(*inputs)
-    return inter.reshape(1, N, L), clean.reshape(1, N, L)
+    return both[0:1], both[1:2]
 
 
 def solution(mesh):

time: 26.4 us -> 21 us (0.80)
  the two profiles are of different devices: /device:TPU:223 before, /device:TPU:225 now
where the time goes in v3:
time: 21 us; the launch traced here: 20.9 us
  Pallas kernels  19 us (90%)
  between operations  1.29 us (6%)
  local copies, waits for them, and re-layouts  0.61 us (3%)
    pallas_call x1, Pallas kernels, local(): pl.pallas_call(functools.partial(kernel, shots, tms), out_shape=shape, in...  19 us
    slice x1, local copies, waits for them, and re-layouts, local(): return (both[0:1], both[1:2])  0.61 us

profile of v3, /device:TPU:225, one launch (start us, length us, event | category | flops | bytes accessed | tf_op | source)
XLA Modules:
  0.0 20.9 jit_solution(4816954841473226066)
XLA Ops:
  1.3 19.0 %shard_map.122 = bf16[2,64,128]{2,1,0:T(8,128)(2,1)S(1)} custom-call(bf16[64,128]{1,0:T(8,128)(2,1)} %bitcast.4, s32[1,64]{1,0:T(1,128)} %live_hbm.1, s32[32]{0:T(128)} %dith_hbm.1, bf16[9,33]{1,0:T(8,128)(2,1)} %des_hbm.1, bf16[30,64]{1,0:T(8,128)(2,1)} %bitcast.5, f32[1,64]{1,0:T(1,128)} %bitcast.6, bf16[3,64,192]{2,1,0:T(8,128)(2,1)} %hw_hbm.1, ...), custom_call_target="tpu_custom_call" | custom-call | tf_op jit(solution)/shard_map/pallas_call | solution.py:381
  20.3 0.6 %fusion = (bf16[1,64,128]{2,1,0:T(8,128)(2,1)}, bf16[1,64,128]{2,1,0:T(8,128)(2,1)}) fusion(bf16[2,64,128]{2,1,0:T(8,128)(2,1)S(1)} %shard_map.122), kind=kLoop, calls=%fused_computation | loop fusion | bytes 65536 | tf_op jit(solution)/shard_map/slice | solution.py:414

commit v4 on v3

--- a/solution.py
+++ b/solution.py
@@ -92,6 +92,7 @@
     tm_recv,
     shot_send,
     shot_recv,
+    near_sem,
 ):
     s, z = lax.axis_index("shot"), lax.axis_index("tm")
     has_left, has_right = z > 0, z < tms - 1
@@ -105,8 +106,6 @@
         (has_right, (s, z + 1)),
         (has_before, (s - 1, z)),
         (has_after, (s + 1, z)),
-        (has_before2, (s - 2, z)),
-        (has_after2, (s + 2, z)),
     ):
         @pl.when(here)
         def _(device=device):
@@ -150,9 +149,6 @@
         c1[a, L:, 0:L] = far
         c1[a, L:, L:] = near
 
-    fetches[0].wait()
-    circulants(des[...], keep_first)
-
     pl.semaphore_wait(barrier, expected)
 
     @pl.when(has_right)
@@ -163,8 +159,14 @@
     def _():
         to_left.start()
 
-    for fetch in fetches[1:]:
+    @pl.when(has_before & has_after)
+    def _():
+        pl.semaphore_signal(near_sem.at[0], inc=1, device_id=(s - 1, z), device_id_type=MESH)
+        pl.semaphore_signal(near_sem.at[1], inc=1, device_id=(s + 1, z), device_id_type=MESH)
+
+    for fetch in fetches:
         fetch.wait()
+    circulants(des[...], keep_first)
 
     lane = iota((1, L), 1)
     left_f, right_f = jnp.where(has_left, 1.0, 0.0), jnp.where(has_right, 1.0, 0.0)
@@ -211,9 +213,11 @@
 
     win[0] = jnp.where((column * time_ok) > 0.0, filter_with(xs, c1), 0.0).astype(BF)
 
-    for copy, there, _ in shot_copies:
+    for i, (copy, there, _) in enumerate(shot_copies):
         @pl.when(there)
-        def _(copy=copy):
+        def _(i=i, copy=copy):
+            if i < 2:
+                pl.semaphore_wait(near_sem.at[i], 1)
             copy.start()
 
     lanes2 = iota((1, 2 * L), 1)
@@ -322,7 +326,7 @@
                 ref[u + step] = act[m * N : (m + 1) * N, L:]
         return keep
 
-    out_bias = ob[0]
+    out_bias = ob[...]
     sixteen = lax.shift_right_logical(lane, 4)
 
     def last(us, step, act):
@@ -374,10 +378,10 @@
         hidden_weights,
         hidden_bias,
         out_weights.reshape(1, CH),
-        out_bias,
+        out_bias.reshape(1, 1),
         shaping,
     )
-    spaces = [pltpu.SMEM if i in (2, 9) else pltpu.VMEM for i in range(len(inputs))]
+    spaces = [pltpu.SMEM if i == 2 else pltpu.VMEM for i in range(len(inputs))]
     both = pl.pallas_call(
         functools.partial(kernel, shots, tms),
         out_shape=shape,
@@ -406,6 +410,7 @@
             pltpu.SemaphoreType.DMA((2,)),
             pltpu.SemaphoreType.DMA((4,)),
             pltpu.SemaphoreType.DMA((4,)),
+            pltpu.SemaphoreType.REGULAR((2,)),
         ],
         compiler_params=pltpu.CompilerParams(
             collective_id=0, has_side_effects=True, vmem_limit_bytes=61 * 1024 * 1024

time: 21 us -> 20.1 us (0.957)
  Pallas kernels: 19 us -> 18.1 us
    pallas_call x1, Pallas kernels: 19 us -> 18.1 us  [local(): pl.pallas_call(functools.partial(kernel, shots, tms), out_shape=shape, in...]
where the time goes in v4:
time: 20.1 us; the launch traced here: 20 us
  Pallas kernels  18.1 us (90%)
  between operations  1.29 us (6%)
  local copies, waits for them, and re-layouts  0.61 us (3%)
    pallas_call x1, Pallas kernels, local(): pl.pallas_call(functools.partial(kernel, shots, tms), out_shape=shape, in...  18.1 us
    slice x1, local copies, waits for them, and re-layouts, local(): return (both[0:1], both[1:2])  0.61 us

profile of v4, /device:TPU:225, one launch (start us, length us, event | category | flops | bytes accessed | tf_op | source)
XLA Modules:
  0.0 20.0 jit_solution(3789980063073576780)
XLA Ops:
  1.3 18.1 %shard_map.122 = bf16[2,64,128]{2,1,0:T(8,128)(2,1)S(1)} custom-call(bf16[64,128]{1,0:T(8,128)(2,1)} %bitcast.6, s32[1,64]{1,0:T(1,128)} %live_hbm.1, s32[32]{0:T(128)} %dith_hbm.1, bf16[9,33]{1,0:T(8,128)(2,1)} %des_hbm.1, bf16[30,64]{1,0:T(8,128)(2,1)} %bitcast.7, f32[1,64]{1,0:T(1,128)} %bitcast.8, bf16[3,64,192]{2,1,0:T(8,128)(2,1)} %hw_hbm.1, ...), custom_call_target="tpu_custom_call" | custom-call | tf_op jit(solution)/shard_map/pallas_call | solution.py:385
  19.4 0.6 %fusion = (bf16[1,64,128]{2,1,0:T(8,128)(2,1)}, bf16[1,64,128]{2,1,0:T(8,128)(2,1)}) fusion(bf16[2,64,128]{2,1,0:T(8,128)(2,1)S(1)} %shard_map.122), kind=kLoop, calls=%fused_computation | loop fusion | bytes 65536 | tf_op jit(solution)/shard_map/slice | solution.py:419

commit v5 on v4

--- a/solution.py
+++ b/solution.py
@@ -72,6 +72,8 @@
     ob,
     shp,
     halos,
+    inner,
+    outer,
     win,
     xs,
     c1,
@@ -130,18 +132,14 @@
     to_right = remote(rec_hbm, halos.at[0], tm_send.at[0], tm_recv.at[0], (s, z + 1))
     to_left = remote(rec_hbm, halos.at[1], tm_send.at[1], tm_recv.at[1], (s, z - 1))
 
-    def to_shot(index, offset):
+    def to_shot(index, offset, part):
         return remote(
-            win.at[0], win.at[SLOT[-offset]], shot_send.at[index], shot_recv.at[index], (s + offset, z))
-
-    shot_copies = [
-        (to_shot(i, offset), there, behind)
-        for i, (offset, there, behind) in enumerate((
-            (2, has_after2, has_before2),
-            (-2, has_before2, has_after2),
-            (1, has_after, has_before),
-            (-1, has_before, has_after)))
-    ]
+            part.at[0], part.at[SLOT[-offset]], shot_send.at[index], shot_recv.at[index], (s + offset, z))
+
+    reach = ((2, has_after2, has_before2), (-2, has_before2, has_after2), (1, has_after, has_before),
+             (-1, has_before, has_after))
+    inner_copies = [(to_shot(i, o, inner), there, behind) for i, (o, there, behind) in enumerate(reach)]
+    outer_copies = [(to_shot(4 + i, o, outer), there, behind) for i, (o, there, behind) in enumerate(reach)]
 
     def keep_first(a, near, far):
         c1[a, 0:L, 0:L] = near
@@ -193,39 +191,53 @@
         even, odd = b0s[pl.ds(16 - 2 * pair, 256), :], b0s[pl.ds(15 - 2 * pair, 256), :]
         w0[:, pair * L : (pair + 1) * L] = jnp.where(upper, odd, even).astype(BF)
 
-    @pl.when(has_left)
-    def _():
-        to_right.wait_recv()
-
-    @pl.when(has_right)
-    def _():
-        to_left.wait_recv()
-
-    sides = jnp.where(lane < 80, halos[1].astype(F32), halos[0].astype(F32))
-    xs[8:72, L:] = jnp.where(alive_halo, sides, 0.0)
-
-    def filter_with(source, matrices):
-        total = None
+    def filter_with(source, half, matrices, total=None):
+        part = slice(half * L, half * L + L)
         for a in range(FN):
-            term = dot_nn(source[pl.ds(4 + a, N), :].astype(BF), matrices[a])
+            term = dot_nn(source[pl.ds(4 + a, N), part].astype(BF), matrices[a, part, :])
             total = term if total is None else total + term
         return total
 
-    win[0] = jnp.where((column * time_ok) > 0.0, filter_with(xs, c1), 0.0).astype(BF)
-
-    for i, (copy, there, _) in enumerate(shot_copies):
+    started = filter_with(xs, 0, c1)
+    inner[0] = jnp.where(alive, started[:, 0:L], 0.0).astype(BF)
+    for i, (copy, there, _) in enumerate(inner_copies):
         @pl.when(there)
         def _(i=i, copy=copy):
             if i < 2:
                 pl.semaphore_wait(near_sem.at[i], 1)
             copy.start()
 
+    @pl.when(has_left)
+    def _():
+        to_right.wait_recv()
+
+    @pl.when(has_right)
+    def _():
+        to_left.wait_recv()
+
+    sides = jnp.where(lane < 80, halos[1].astype(F32), halos[0].astype(F32))
+    xs[8:72, L:] = jnp.where(alive_halo, sides, 0.0)
+    own = jnp.where((column * time_ok) > 0.0, filter_with(xs, 1, c1, started), 0.0)
+    spare = (lane >= 64) & (lane < 96)
+    outer[0] = jnp.where(spare, pltpu.roll(own[:, 0:L], L - 48, 1), own[:, L:]).astype(BF)
+    for copy, there, _ in outer_copies:
+        @pl.when(there)
+        def _(copy=copy):
+            copy.start()
+
+    win[...] = own.astype(BF)
+
     lanes2 = iota((1, 2 * L), 1)
 
     def make_planes(offset, there):
-        values = win[SLOT[offset]].astype(F32)
-        if there is not None:
-            values = jnp.where(there, values, 0.0)
+        if offset == 0:
+            values = win[...].astype(F32)
+        else:
+            slot = SLOT[offset]
+            rim = outer[slot].astype(F32)
+            middle = (lane >= 16) & (lane < 112)
+            centre = jnp.where(middle, inner[slot].astype(F32), pltpu.roll(rim, 48, 1))
+            values = jnp.where(there, jnp.concatenate([centre, rim], axis=1), 0.0)
         a = offset + SHOT_TAPS // 2
         planes[a] = pltpu.roll(values, GAP * a + 33, 1).astype(BF)
         p = a + SHOT_TAPS
@@ -268,25 +280,36 @@
         c2[a, L:, :] = far
 
     circulants(shp[...], keep_second)
-    for i, offset in ((2, -1), (3, 1), (0, -2), (1, 2)):
-        copy, _, behind = shot_copies[i]
+    def merge(numbers, begin, last):
+        for part in range(2):
+            rows = slice(part * 32, part * 32 + 32)
+            held = {p: planes[p, rows, :] for p in numbers}
+            for g in range(GROUPS):
+                place = ((lanes2 - 16 * g) & 255).astype(F32).astype(BF)
+                merged = held[numbers[0]] if begin else gs[g, rows, :]
+                for p in numbers[1:] if begin else numbers:
+                    inside = (place >= GAP * p) & (place < GAP * p + GAP)
+                    merged = jnp.where(inside, held[p], merged)
+                if last and g:
+                    merged = pltpu.roll(merged.astype(F32), 256 - 16 * g, 1).astype(BF)
+                gs[g, rows, :] = merged
+
+    def arrived(i, offset):
+        inside, _, behind = inner_copies[i]
+        beyond = outer_copies[i][0]
 
         @pl.when(behind)
-        def _(copy=copy):
-            copy.wait_recv()
+        def _():
+            inside.wait_recv()
+            beyond.wait_recv()
         make_planes(offset, behind)
 
-    for part in range(2):
-        rows = slice(part * 32, part * 32 + 32)
-        held = [planes[p, rows, :].astype(F32) for p in range(2 * SHOT_TAPS)]
-        for g in range(GROUPS):
-            place = (lanes2 - 16 * g) & 255
-            merged = held[0]
-            for p in range(1, 2 * SHOT_TAPS):
-                merged = jnp.where(place >= GAP * p, held[p], merged)
-            if g:
-                merged = pltpu.roll(merged, 256 - 16 * g, 1)
-            gs[g, rows, :] = merged.astype(BF)
+    arrived(2, -1)
+    arrived(3, 1)
+    merge((1, 2, 3, 6, 7, 8), True, False)
+    arrived(0, -2)
+    arrived(1, 2)
+    merge((0, 4, 5, 9), False, True)
 
     def finish(total, bias, factor):
         act = jnp.maximum(total + bias, 0.0)
@@ -347,16 +370,16 @@
     out[0] = middle.astype(BF)
     edge = jnp.where(lane < 80, pred[10], pred[1])
     edge = jnp.where(alive_halo, edge, 0.0)
-    rest = (win[0].astype(F32) - jnp.concatenate([middle, edge], axis=1)).astype(BF).astype(F32)
+    rest = (win[...].astype(F32) - jnp.concatenate([middle, edge], axis=1)).astype(BF).astype(F32)
     ds[0:8, :] = jnp.zeros((8, 2 * L), F32)
     ds[72:80, :] = jnp.zeros((8, 2 * L), F32)
     ds[8:72, :] = rest
-    out[1] = jnp.where(alive, filter_with(ds, c2), 0.0).astype(BF)
+    out[1] = jnp.where(alive, filter_with(ds, 1, c2, filter_with(ds, 0, c2)), 0.0).astype(BF)
 
     for here, copy in (
         (has_right, to_right),
         (has_left, to_left),
-        *[(there, copy) for copy, there, _ in shot_copies],
+        *[(there, copy) for copy, there, _ in inner_copies + outer_copies],
     ):
         @pl.when(here)
         def _(copy=copy):
@@ -390,7 +413,9 @@
         scratch_shapes=[
             *[space(x.shape, x.dtype) for space, x in zip(spaces, inputs)],
             pltpu.VMEM((2, N, L), BF),
-            pltpu.VMEM((5, N, 2 * L), BF),
+            pltpu.VMEM((5, N, L), BF),
+            pltpu.VMEM((5, N, L), BF),
+            pltpu.VMEM((N, 2 * L), BF),
             pltpu.VMEM((80, 2 * L), F32),
             pltpu.VMEM((FN, 2 * L, 2 * L), BF),
             pltpu.VMEM((FN, 2 * L, L), BF),
@@ -408,8 +433,8 @@
             pltpu.SemaphoreType.DMA((len(inputs),)),
             pltpu.SemaphoreType.DMA((2,)),
             pltpu.SemaphoreType.DMA((2,)),
-            pltpu.SemaphoreType.DMA((4,)),
-            pltpu.SemaphoreType.DMA((4,)),
+            pltpu.SemaphoreType.DMA((8,)),
+            pltpu.SemaphoreType.DMA((8,)),
             pltpu.SemaphoreType.REGULAR((2,)),
         ],
         compiler_params=pltpu.CompilerParams(

time: 20.1 us -> 20.2 us (level)
  no operation moved by 1% of the time
where the time goes in v5:
time: 20.2 us; the launch traced here: 20 us
  Pallas kernels  18.1 us (90%)
  between operations  1.29 us (6%)
  local copies, waits for them, and re-layouts  0.61 us (3%)
    pallas_call x1, Pallas kernels, local(): pl.pallas_call(functools.partial(kernel, shots, tms), out_shape=shape, in...  18.1 us
    slice x1, local copies, waits for them, and re-layouts, local(): return (both[0:1], both[1:2])  0.61 us

profile of v5, /device:TPU:225, one launch (start us, length us, event | category | flops | bytes accessed | tf_op | source)
XLA Modules:
  0.0 20.0 jit_solution(8813885198291935823)
XLA Ops:
  1.3 18.1 %shard_map.122 = bf16[2,64,128]{2,1,0:T(8,128)(2,1)S(1)} custom-call(bf16[64,128]{1,0:T(8,128)(2,1)} %bitcast.6, s32[1,64]{1,0:T(1,128)} %live_hbm.1, s32[32]{0:T(128)} %dith_hbm.1, bf16[9,33]{1,0:T(8,128)(2,1)} %des_hbm.1, bf16[30,64]{1,0:T(8,128)(2,1)} %bitcast.7, f32[1,64]{1,0:T(1,128)} %bitcast.8, bf16[3,64,192]{2,1,0:T(8,128)(2,1)} %hw_hbm.1, ...), custom_call_target="tpu_custom_call" | custom-call | tf_op jit(solution)/shard_map/pallas_call | solution.py:408
  19.4 0.6 %fusion = (bf16[1,64,128]{2,1,0:T(8,128)(2,1)}, bf16[1,64,128]{2,1,0:T(8,128)(2,1)}) fusion(bf16[2,64,128]{2,1,0:T(8,128)(2,1)S(1)} %shard_map.122), kind=kLoop, calls=%fused_computation | loop fusion | bytes 65536 | tf_op jit(solution)/shard_map/slice | solution.py:444

commit v6 on v5

--- a/solution.py
+++ b/solution.py
@@ -149,13 +149,13 @@
 
     pl.semaphore_wait(barrier, expected)
 
+    @pl.when(has_left)
+    def _():
+        to_left.start()
+
     @pl.when(has_right)
     def _():
         to_right.start()
-
-    @pl.when(has_left)
-    def _():
-        to_left.start()
 
     @pl.when(has_before & has_after)
     def _():
@@ -192,7 +192,7 @@
         w0[:, pair * L : (pair + 1) * L] = jnp.where(upper, odd, even).astype(BF)
 
     def filter_with(source, half, matrices, total=None):
-        part = slice(half * L, half * L + L)
+        part = slice(0, 2 * L) if half is None else slice(half * L, half * L + L)
         for a in range(FN):
             term = dot_nn(source[pl.ds(4 + a, N), part].astype(BF), matrices[a, part, :])
             total = term if total is None else total + term
@@ -200,7 +200,9 @@
 
     started = filter_with(xs, 0, c1)
     inner[0] = jnp.where(alive, started[:, 0:L], 0.0).astype(BF)
-    for i, (copy, there, _) in enumerate(inner_copies):
+    for i in (1, 3, 0, 2):
+        copy, there, _ = inner_copies[i]
+
         @pl.when(there)
         def _(i=i, copy=copy):
             if i < 2:
@@ -220,7 +222,9 @@
     own = jnp.where((column * time_ok) > 0.0, filter_with(xs, 1, c1, started), 0.0)
     spare = (lane >= 64) & (lane < 96)
     outer[0] = jnp.where(spare, pltpu.roll(own[:, 0:L], L - 48, 1), own[:, L:]).astype(BF)
-    for copy, there, _ in outer_copies:
+    for i in (1, 3, 0, 2):
+        copy, there, _ = outer_copies[i]
+
         @pl.when(there)
         def _(copy=copy):
             copy.start()
@@ -357,9 +361,9 @@
             r = m % step
             a3[u // 8 - 1, :, 2 * L * r : 2 * L * (r + 1)] = act[m * N : (m + 1) * N]
 
-    layer(a0, into(a1), 0, 1, 47, 8)
-    layer(a1, into(a2), 1, 1, 23, 4)
-    layer(a2, last, 2, 1, 11, 2)
+    layer(a0, into(a1), 0, 1, 47, 4)
+    layer(a1, into(a2), 1, 1, 23, 2)
+    layer(a2, last, 2, 1, 11, 1)
     scores = (dot_nn(a3[...].reshape(10 * N, 8 * L), wo[...]) + out_bias).astype(BF).astype(F32)
     pred = {j: scores[(j - 1) * N : j * N] for j in range(1, 11)}
 
@@ -374,7 +378,7 @@
     ds[0:8, :] = jnp.zeros((8, 2 * L), F32)
     ds[72:80, :] = jnp.zeros((8, 2 * L), F32)
     ds[8:72, :] = rest
-    out[1] = jnp.where(alive, filter_with(ds, 1, c2, filter_with(ds, 0, c2)), 0.0).astype(BF)
+    out[1] = jnp.where(alive, filter_with(ds, None, c2), 0.0).astype(BF)
 
     for here, copy in (
         (has_right, to_right),

time: 20.2 us -> 20 us (0.990)
  no operation moved by 1% of the time
where the time goes in v6:
time: 20 us; the launch traced here: 19.8 us
  Pallas kernels  17.9 us (89%)
  between operations  1.29 us (6%)
  local copies, waits for them, and re-layouts  0.61 us (3%)
    pallas_call x1, Pallas kernels, local(): pl.pallas_call(functools.partial(kernel, shots, tms), out_shape=shape, in...  17.9 us
    slice x1, local copies, waits for them, and re-layouts, local(): return (both[0:1], both[1:2])  0.61 us

profile of v6, /device:TPU:225, one launch (start us, length us, event | category | flops | bytes accessed | tf_op | source)
XLA Modules:
  0.0 19.8 jit_solution(18212070499470046275)
XLA Ops:
  1.3 17.9 %shard_map.122 = bf16[2,64,128]{2,1,0:T(8,128)(2,1)S(1)} custom-call(bf16[64,128]{1,0:T(8,128)(2,1)} %bitcast.6, s32[1,64]{1,0:T(1,128)} %live_hbm.1, s32[32]{0:T(128)} %dith_hbm.1, bf16[9,33]{1,0:T(8,128)(2,1)} %des_hbm.1, bf16[30,64]{1,0:T(8,128)(2,1)} %bitcast.7, f32[1,64]{1,0:T(1,128)} %bitcast.8, bf16[3,64,192]{2,1,0:T(8,128)(2,1)} %hw_hbm.1, ...), custom_call_target="tpu_custom_call" | custom-call | tf_op jit(solution)/shard_map/pallas_call | solution.py:412
  19.2 0.6 %fusion = (bf16[1,64,128]{2,1,0:T(8,128)(2,1)}, bf16[1,64,128]{2,1,0:T(8,128)(2,1)}) fusion(bf16[2,64,128]{2,1,0:T(8,128)(2,1)S(1)} %shard_map.122), kind=kLoop, calls=%fused_computation | loop fusion | bytes 65536 | tf_op jit(solution)/shard_map/slice | solution.py:448

commit v7 on v4

--- a/solution.py
+++ b/solution.py
@@ -151,13 +151,13 @@
 
     pl.semaphore_wait(barrier, expected)
 
+    @pl.when(has_left)
+    def _():
+        to_left.start()
+
     @pl.when(has_right)
     def _():
         to_right.start()
-
-    @pl.when(has_left)
-    def _():
-        to_left.start()
 
     @pl.when(has_before & has_after)
     def _():
@@ -213,7 +213,9 @@
 
     win[0] = jnp.where((column * time_ok) > 0.0, filter_with(xs, c1), 0.0).astype(BF)
 
-    for i, (copy, there, _) in enumerate(shot_copies):
+    for i in (1, 3, 0, 2):
+        copy, there, _ = shot_copies[i]
+
         @pl.when(there)
         def _(i=i, copy=copy):
             if i < 2:
@@ -268,6 +270,20 @@
         c2[a, L:, :] = far
 
     circulants(shp[...], keep_second)
+    def merge(numbers, begin, last):
+        for part in range(2):
+            rows = slice(part * 32, part * 32 + 32)
+            held = {p: planes[p, rows, :] for p in numbers}
+            for g in range(GROUPS):
+                place = ((lanes2 - 16 * g) & 255).astype(F32).astype(BF)
+                merged = held[numbers[0]] if begin else gs[g, rows, :]
+                for p in numbers[1:] if begin else numbers:
+                    inside = (place >= GAP * p) & (place < GAP * p + GAP)
+                    merged = jnp.where(inside, held[p], merged)
+                if last and g:
+                    merged = pltpu.roll(merged.astype(F32), 256 - 16 * g, 1).astype(BF)
+                gs[g, rows, :] = merged
+
     for i, offset in ((2, -1), (3, 1), (0, -2), (1, 2)):
         copy, _, behind = shot_copies[i]
 
@@ -275,18 +291,10 @@
         def _(copy=copy):
             copy.wait_recv()
         make_planes(offset, behind)
-
-    for part in range(2):
-        rows = slice(part * 32, part * 32 + 32)
-        held = [planes[p, rows, :].astype(F32) for p in range(2 * SHOT_TAPS)]
-        for g in range(GROUPS):
-            place = (lanes2 - 16 * g) & 255
-            merged = held[0]
-            for p in range(1, 2 * SHOT_TAPS):
-                merged = jnp.where(place >= GAP * p, held[p], merged)
-            if g:
-                merged = pltpu.roll(merged, 256 - 16 * g, 1)
-            gs[g, rows, :] = merged.astype(BF)
+        if offset == 1:
+            merge((1, 2, 3, 6, 7, 8), True, False)
+
+    merge((0, 4, 5, 9), False, True)
 
     def finish(total, bias, factor):
         act = jnp.maximum(total + bias, 0.0)
@@ -334,9 +342,9 @@
             r = m % step
             a3[u // 8 - 1, :, 2 * L * r : 2 * L * (r + 1)] = act[m * N : (m + 1) * N]
 
-    layer(a0, into(a1), 0, 1, 47, 8)
-    layer(a1, into(a2), 1, 1, 23, 4)
-    layer(a2, last, 2, 1, 11, 2)
+    layer(a0, into(a1), 0, 1, 47, 4)
+    layer(a1, into(a2), 1, 1, 23, 2)
+    layer(a2, last, 2, 1, 11, 1)
     scores = (dot_nn(a3[...].reshape(10 * N, 8 * L), wo[...]) + out_bias).astype(BF).astype(F32)
     pred = {j: scores[(j - 1) * N : j * N] for j in range(1, 11)}
 

time: 20.1 us -> 19.9 us (0.990)
  Pallas kernels: 18.1 us -> 17.8 us
    pallas_call x1, Pallas kernels: 18.1 us -> 17.8 us  [local(): pl.pallas_call(functools.partial(kernel, shots, tms), out_shape=shape, in...]
where the time goes in v7:
time: 19.9 us; the launch traced here: 19.7 us
  Pallas kernels  17.8 us (89%)
  between operations  1.29 us (6%)
  local copies, waits for them, and re-layouts  0.61 us (3%)
    pallas_call x1, Pallas kernels, local(): pl.pallas_call(functools.partial(kernel, shots, tms), out_shape=shape, in...  17.8 us
    slice x1, local copies, waits for them, and re-layouts, local(): return (both[0:1], both[1:2])  0.61 us

profile of v7, /device:TPU:225, one launch (start us, length us, event | category | flops | bytes accessed | tf_op | source)
XLA Modules:
  0.0 19.7 jit_solution(6343446527544479059)
XLA Ops:
  1.3 17.8 %shard_map.122 = bf16[2,64,128]{2,1,0:T(8,128)(2,1)S(1)} custom-call(bf16[64,128]{1,0:T(8,128)(2,1)} %bitcast.6, s32[1,64]{1,0:T(1,128)} %live_hbm.1, s32[32]{0:T(128)} %dith_hbm.1, bf16[9,33]{1,0:T(8,128)(2,1)} %des_hbm.1, bf16[30,64]{1,0:T(8,128)(2,1)} %bitcast.7, f32[1,64]{1,0:T(1,128)} %bitcast.8, bf16[3,64,192]{2,1,0:T(8,128)(2,1)} %hw_hbm.1, ...), custom_call_target="tpu_custom_call" | custom-call | tf_op jit(solution)/shard_map/pallas_call | solution.py:393
  19.1 0.6 %fusion = (bf16[1,64,128]{2,1,0:T(8,128)(2,1)}, bf16[1,64,128]{2,1,0:T(8,128)(2,1)}) fusion(bf16[2,64,128]{2,1,0:T(8,128)(2,1)S(1)} %shard_map.122), kind=kLoop, calls=%fused_computation | loop fusion | bytes 65536 | tf_op jit(solution)/shard_map/slice | solution.py:427
